TPU v7x, 256 devices: a whole 4x4x8 slice. The times are simulated.
256 devices in a mesh: grp: 2 (over core), gx: 32 (over z, y), gy: 4 (over x).
Axes of the slice: x: 4, y: 4, z: 8, core: 2. Of those that a mesh axis runs over, the one named last changes fastest.
Arguments:
- gas_state: float32 [5, 256, 96, 512], P(None, 'gx', 'grp', 'gy'), may hold values from -0.5 to 3.5, as said below
- droplets: float32 [8, 4194304], P(None, ('grp', 'gx', 'gy')), may hold values from -1 to 7, as said below
- bin_blocks: int32 [32768], P(('grp', 'gx', 'gy')), may hold values from 0 to 95, as said below
- bin_counts: int32 [32768], P(('grp', 'gx', 'gy')), may hold values from 16 to 128, as said below
- crossing: int32 [2, 65536], P(None, ('grp', 'gx', 'gy')), may hold values from 0 to 16383, as said below
Outputs:
- gas_next: float32 [5, 256, 96, 512], P(None, 'gx', 'grp', 'gy')
- droplets_next: float32 [8, 4194304], P(None, ('grp', 'gx', 'gy'))
- arrivals: float32 [8, 2, 65536], P(None, None, ('grp', 'gx', 'gy'))
Inputs may be any that keep to these rules, and one draw needn't show every extreme that they name: `gas_state`: component 0 (density) lies in [0.8, 1.2], components 1 to 3 in [-0.5, 0.5], component 4 in [2.5, 3.5]. `droplets`: rows 0 to 2 lie in [0, 7], rows 3 to 5 in [-1, 1], row 6 in [0.5, 2], row 7 in [0.5, 1.5], in every slot. `bin_blocks`: the 4 entries of one device for one gx slab are distinct. `bin_counts`: every device has a bin with 128 live droplets. `crossing`: all 512 entries of one device are distinct slots of live droplets.
All inputs are finite; a program needn't handle non-finite values.
Results may differ from a plain program's by a relative error of at most 0.00014.
Values sent between devices are 32-bit elements; how exact they have to be, the bound alone decides.
No kernel may reach another device: no remote copies, remote signals or barrier semaphores. Data moves between devices by JAX's collectives and lax.ppermute only.
A program may use at most 128 MiB of HBM per device.

v0:
```python
import jax
import jax.numpy as jnp
from jax import lax
from jax.experimental import pallas as pl
from jax.experimental.pallas import tpu as pltpu
from jax.sharding import PartitionSpec as P

f32 = jnp.float32
bf16 = jnp.bfloat16

peers = 32
per_peer = 4
bins = 128
lanes = 128
blocks = 96
depth, across, height = 8, 48, 128
plane = depth * across
chunk_rows = per_peer * 8 + 1
moving = 256

vmem = pl.BlockSpec(memory_space=pltpu.VMEM)
smem = pl.BlockSpec(memory_space=pltpu.SMEM)


def params(mib):
    return pltpu.CompilerParams(vmem_limit_bytes=mib * 1024 * 1024)


def lane_index(rows):
    return lax.broadcasted_iota(jnp.int32, (rows, lanes), 1)


def split(x):
    high = x.astype(bf16)
    return high, (x - high.astype(f32)).astype(bf16)


def pack_kernel(drops, ids, counts, out):
    lane = lane_index(1)
    for p in range(peers):
        out[p * chunk_rows : p * chunk_rows + 32, :] = drops[p * 32 : (p + 1) * 32, :]
        row = jnp.zeros((1, lanes), jnp.int32)
        for r in range(per_peer):
            row = jnp.where(lane == r, ids[p * per_peer + r], row)
            row = jnp.where(lane == per_peer + r, counts[p * per_peer + r], row)
        out[p * chunk_rows + 32 : (p + 1) * chunk_rows, :] = row.astype(f32)


def face_kernel(gas, x_low, x_high, z_both, y_low, y_high):
    for v in range(5):
        x_low[v * across : (v + 1) * across, :] = gas[v * plane : v * plane + across, :]
        x_high[v * across : (v + 1) * across, :] = gas[(v + 1) * plane - across : (v + 1) * plane, :]
        z_both[v * 8 : (v + 1) * 8, :] = gas[pl.ds(v * plane, 8, stride=across), :]
        z_both[40 + v * 8 : 40 + (v + 1) * 8, :] = gas[pl.ds(v * plane + across - 1, 8, stride=across), :]
    row = lax.broadcasted_iota(jnp.int32, (8, lanes), 0)
    lane = lane_index(8)
    pick = jnp.where((row == 0) & (lane == 0) | (row == 1) & (lane == lanes - 1), 1.0, 0.0).astype(f32)
    ends = lax.dot_general(
        pick, gas[...], (((1,), (1,)), ((), ())),
        precision=lax.Precision.HIGHEST, preferred_element_type=f32,
    )
    y_low[...] = ends[0:1]
    y_high[...] = ends[1:2]


def table_kernel(gas, out, padded):
    padded[0 : 5 * plane, :] = gas[...]
    padded[5 * plane :, :] = jnp.zeros((3 * plane, lanes), f32)
    lane = lane_index(64)
    group = (lane >> 3) & 7
    first = lane < 64

    def strip(bz, carry):
        for by in range(8):
            pair = jnp.zeros((64, lanes), f32)
            for j in range(8):
                tiles = [
                    padded[pl.ds(i * across + bz * 8 + j, 8, stride=plane), :] for i in range(8)
                ]
                layer = jnp.concatenate(tiles, axis=0)
                shift = (j - by) * 8 % lanes
                if shift:
                    layer = pltpu.roll(layer, shift, 1)
                pair = jnp.where(group == j, layer, pair)
            other = pltpu.roll(pair, 64, 1)
            for number, block in ((by, jnp.where(first, pair, other)), (by + 8, jnp.where(first, other, pair))):
                high, low = split(block)
                start = pl.multiple_of((bz * 16 + number) * 128, 128)
                out[pl.ds(start, 64), :] = high
                out[pl.ds(start + 64, 64), :] = low
        return carry

    lax.fori_loop(0, 6, strip, 0)


def hats(tile):
    node = lax.broadcasted_iota(jnp.int32, (8, lanes), 0).astype(f32)
    return [jnp.maximum(0.0, 1.0 - jnp.abs(tile[a : a + 1] - node)) for a in range(3)]


def pair_weights(hat_z, hat_y):
    high, low = split(jnp.concatenate([hat_z[j : j + 1] * hat_y for j in range(8)], axis=0))
    return jnp.concatenate([high, low], axis=0)


def sample_kernel(received, table, results, drops, index, index_smem, sampled, sem):
    for p in range(peers):
        index[p : p + 1, :] = received[p * chunk_rows + 32 : (p + 1) * chunk_rows, :].astype(jnp.int32)
    copy = pltpu.make_async_copy(index, index_smem, sem)
    copy.start()
    for p in range(peers):
        drops[p * 32 : (p + 1) * 32, :] = received[p * chunk_rows : p * chunk_rows + 32, :]
    copy.wait()

    def group(g, carry):
        base = pl.multiple_of(g * 64, 64)
        for b in range(8):
            hat_x, hat_z, hat_y = hats(drops[pl.ds(base + b * 8, 8), :])
            block = index_smem[g * 2 + b // 4, b % 4]
            rows = table[pl.ds(pl.multiple_of(block * 128, 128), 128), :]
            product = jnp.dot(rows, pair_weights(hat_z, hat_y), preferred_element_type=f32)
            total = None
            for i in range(8):
                part = (product[i * 8 : i * 8 + 8] + product[64 + i * 8 : 72 + i * 8]) * hat_x[i : i + 1]
                total = part if total is None else total + part
            sampled[b * 8 : (b + 1) * 8, :] = total
        density, m1, m2, m3, energy = [sampled[pl.ds(v, 8, stride=8), :] for v in range(5)]
        v1, v2, v3, mass, heat = [drops[pl.ds(base + n, 8, stride=8), :] for n in range(3, 8)]
        inverse = 1.0 / density
        u1, u2, u3 = m1 * inverse, m2 * inverse, m3 * inverse
        gas_heat = 0.4 * (energy - 0.5 * (m1 * u1 + m2 * u2 + m3 * u3)) * inverse
        inverse_area = jnp.exp(jnp.log(mass) * (-2.0 / 3.0))
        rate = density * inverse_area * -0.8
        drag = jnp.exp(rate)
        values = [
            u1 + (v1 - u1) * drag,
            u2 + (v2 - u2) * drag,
            u3 + (v3 - u3) * drag,
            mass * jnp.exp(-0.2 * gas_heat * heat * inverse_area),
            gas_heat + (heat - gas_heat) * jnp.exp(rate * (1.0 / 1.5)),
        ]
        for n in range(5):
            results[pl.ds(g * 40 + n, 8, stride=5), :] = values[n]
        return carry

    lax.fori_loop(0, bins // 8, group, 0)


def primitives(s):
    inverse = 1.0 / s[0]
    u = [s[1] * inverse, s[2] * inverse, s[3] * inverse]
    pressure = 0.4 * (s[4] - 0.5 * (s[1] * u[0] + s[2] * u[1] + s[3] * u[2]))
    return u, pressure


def flux(s, u, pressure, a):
    normal = u[a]
    out = [s[1 + a]]
    for c in range(3):
        out.append(s[1 + c] * normal + pressure if c == a else s[1 + c] * normal)
    out.append((s[4] + pressure) * normal)
    return out


def gas_kernel(results, drops, index, gas, x_low, x_high, z_both, y_low, y_high, out,
               sums, gains, pairs, sources, y_ends, x_padded, z_flux):
    sums[...] = jnp.zeros(sums.shape, f32)
    lane8 = lane_index(8)

    def group(g, carry):
        base = pl.multiple_of(g * 64, 64)
        v1, v2, v3, mass, heat = [drops[pl.ds(base + n, 8, stride=8), :] for n in range(3, 8)]
        w1, w2, w3, mass_new, heat_new = [results[pl.ds(g * 40 + n, 8, stride=5), :] for n in range(5)]
        values = [
            mass - mass_new,
            mass * v1 - mass_new * w1,
            mass * v2 - mass_new * w2,
            mass * v3 - mass_new * w3,
            0.5 * mass * (v1 * v1 + v2 * v2 + v3 * v3) + mass * heat
            - 0.5 * mass_new * (w1 * w1 + w2 * w2 + w3 * w3) - mass_new * heat_new,
        ]
        for n in range(5):
            gains[pl.ds(n, 8, stride=8), :] = 4.0 * values[n]
        for b in range(8):
            hat_x, hat_z, hat_y = hats(drops[pl.ds(base + b * 8, 8), :])
            peer = g * 2 + b // 4
            block = index[peer, b % 4]
            live = jnp.where(lane8 < index[peer, per_peer + b % 4], gains[b * 8 : (b + 1) * 8, :], 0.0)
            spread = jnp.concatenate([live[v : v + 1] * hat_x for v in range(5)], axis=0)
            high, low = split(spread)
            weights = pair_weights(hat_z, hat_y)
            dims = (((1,), (1,)), ((), ()))
            added = lax.dot_general(high, weights, dims, preferred_element_type=f32)
            added += lax.dot_general(low, weights, dims, preferred_element_type=f32)
            place = pl.ds(pl.multiple_of(block * 40, 8), 40)
            sums[place, :] = sums[place, :] + added
        return carry

    lax.fori_loop(0, bins // 8, group, 0)

    lane40 = lane_index(40)
    chunk = (lane40 >> 3) & 7
    first = lane40 < 64

    def strip(bz, carry):
        for by in range(8):
            near = sums[pl.ds(pl.multiple_of((bz * 16 + by) * 40, 8), 40), :]
            far = sums[pl.ds(pl.multiple_of((bz * 16 + by + 8) * 40, 8), 40), :]
            pairs[by * 40 : (by + 1) * 40, :] = jnp.where(
                first, near + pltpu.roll(near, 64, 1), far + pltpu.roll(far, 64, 1)
            )
        for j in range(8):
            layer = jnp.zeros((40, lanes), f32)
            for by in range(8):
                part = pairs[by * 40 : (by + 1) * 40, :]
                shift = (by - j) * 8 % lanes
                if shift:
                    part = pltpu.roll(part, shift, 1)
                layer = jnp.where(chunk == by, part, layer)
            for v in range(5):
                sources[pl.ds(v * plane + bz * 8 + j, 8, stride=across), :] = layer[v * 8 : (v + 1) * 8]
        return carry

    lax.fori_loop(0, 6, strip, 0)

    row8 = lax.broadcasted_iota(jnp.int32, (8, lanes), 0)
    place = jnp.where((row8 == 0) & (lane8 == 0) | (row8 == 1) & (lane8 == lanes - 1), 1.0, 0.0).astype(f32)
    ends = jnp.concatenate([y_low[...], y_high[...], jnp.zeros((6, 5 * plane), f32)], axis=0)
    y_ends[...] = lax.dot_general(
        ends, place, (((0,), (0,)), ((), ())),
        precision=lax.Precision.HIGHEST, preferred_element_type=f32,
    )
    for v in range(5):
        x_padded[v * 480 : v * 480 + across, :] = x_low[v * across : (v + 1) * across, :]
        x_padded[v * 480 + across : v * 480 + 432, :] = gas[v * plane : (v + 1) * plane, :]
        x_padded[v * 480 + 432 : (v + 1) * 480, :] = x_high[v * across : (v + 1) * across, :]
    for side in range(2):
        edge = [z_both[side * 40 + v * 8 : side * 40 + (v + 1) * 8, :] for v in range(5)]
        edge_flux = flux(edge, *primitives(edge), 1)
        for v in range(5):
            z_flux[side * 40 + v * 8 : side * 40 + (v + 1) * 8, :] = edge_flux[v]

    row = lax.broadcasted_iota(jnp.int32, (across, lanes), 0)
    lane = lane_index(across)

    def layer(i, carry):
        def cells(at):
            return [x_padded[pl.ds(pl.multiple_of(v * 480 + at * across, 8), across), :] for v in range(5)]

        def rows(v):
            return pl.ds(pl.multiple_of(v * plane + i * across, 8), across)

        here, below, above = cells(i + 1), cells(i), cells(i + 2)
        u, pressure = primitives(here)
        flux_above = flux(above, *primitives(above), 0)
        flux_below = flux(below, *primitives(below), 0)
        flux_z = flux(here, u, pressure, 1)
        flux_y = flux(here, u, pressure, 2)
        ends = [y_ends[rows(v), :] for v in range(5)]
        flux_ends = flux(ends, *primitives(ends), 2)
        for v in range(5):
            z_low = z_both[pl.ds(40 + v * 8 + i, 1), :]
            z_high = z_both[pl.ds(v * 8 + i, 1), :]
            z_low_flux = z_flux[pl.ds(40 + v * 8 + i, 1), :]
            z_high_flux = z_flux[pl.ds(v * 8 + i, 1), :]

            def z_pair(x, low, high):
                return (
                    jnp.where(row == 0, low, pltpu.roll(x, 1, 0)),
                    jnp.where(row == across - 1, high, pltpu.roll(x, across - 1, 0)),
                )

            def y_pair(x, end):
                return (
                    jnp.where(lane == 0, end, pltpu.roll(x, 1, 1)),
                    jnp.where(lane == lanes - 1, end, pltpu.roll(x, lanes - 1, 1)),
                )

            z_down, z_up = z_pair(here[v], z_low, z_high)
            z_flux_down, z_flux_up = z_pair(flux_z[v], z_low_flux, z_high_flux)
            y_down, y_up = y_pair(here[v], ends[v])
            y_flux_down, y_flux_up = y_pair(flux_y[v], flux_ends[v])
            spread = (below[v] + above[v]) + (z_down + z_up) + (y_down + y_up) - 6.0 * here[v]
            change = (flux_above[v] - flux_below[v]) + (z_flux_up - z_flux_down) + (y_flux_up - y_flux_down)
            flow = 0.5 * change - 1.5 * spread
            out[rows(v), :] = here[v] - 0.1 * flow + sources[rows(v), :]
        return carry

    lax.fori_loop(0, depth, layer, 0)


def leave_kernel(returned, drops, crossing, updated, toward_next, toward_previous, shifted):
    shifted[0:8, :] = jnp.zeros((8, lanes), f32)
    shifted[8 : 8 + 640, :] = returned[...]
    shifted[648:656, :] = jnp.zeros((8, lanes), f32)
    row = lax.broadcasted_iota(jnp.int32, (8, lanes), 0)
    for b in range(bins):
        speeds = shifted[8 + b * 5 : 16 + b * 5, :]
        values = shifted[5 + b * 5 : 13 + b * 5, :]
        updated[b * 8 : (b + 1) * 8, :] = jnp.where(row < 3, drops[b * 8 : (b + 1) * 8, :] + 0.2 * speeds, values)

    lane = lane_index(8)

    def batch(s, carry):
        tiles = list(carry)
        for t in range(4):
            for e in range(8):
                target = s * 8 + e
                slot = crossing[t // 2, (t % 2) * lanes + target]
                tile = updated[pl.ds(pl.multiple_of((slot >> 7) * 8, 8), 8), :]
                moved = pltpu.roll(tile, (target - slot) & (lanes - 1), 1)
                tiles[t] = jnp.where(lane == target, moved, tiles[t])
        return tuple(tiles)

    tiles = lax.fori_loop(0, lanes // 8, batch, (jnp.zeros((8, lanes), f32),) * 4)
    toward_next[...] = jnp.concatenate(tiles[0:2], axis=1)
    toward_previous[...] = jnp.concatenate(tiles[2:4], axis=1)


def stay_kernel(updated, counts, crossing, out):
    row = lax.broadcasted_iota(jnp.int32, (bins, moving), 0)
    departed = None
    for side in range(2):
        slots = crossing[side : side + 1, :]
        in_bin = jnp.where(row == (slots >> 7), 1.0, 0.0).astype(bf16)
        in_lane = jnp.where(row == (slots & (lanes - 1)), 1.0, 0.0).astype(bf16)
        part = lax.dot_general(in_bin, in_lane, (((1,), (1,)), ((), ())), preferred_element_type=f32)
        departed = part if departed is None else departed + part
    stays = 1.0 - departed
    lane = lane_index(1)
    for b in range(bins):
        keep = jnp.where(lane < counts[b], stays[b : b + 1], 0.0)
        out[b * 8 : (b + 1) * 8, :] = updated[b * 8 : (b + 1) * 8, :] * keep


def shape(rows, columns=lanes, dtype=f32):
    return jax.ShapeDtypeStruct((rows, columns), dtype)


def shifted_by(x, axis, by):
    count = lax.axis_size(axis)
    return lax.ppermute(x, axis, [(i, (i + by) % count) for i in range(count)])


def exchange(x):
    return lax.all_to_all(x, "gx", split_axis=0, concat_axis=0, tiled=True)


def per_device(gas_state, droplets, bin_blocks, bin_counts, crossing):
    gas = gas_state.reshape(5 * plane, lanes)
    drops = droplets.reshape(8, bins, lanes).transpose(1, 0, 2).reshape(bins * 8, lanes)

    packed = pl.pallas_call(
        pack_kernel, out_shape=shape(peers * chunk_rows), in_specs=[vmem, smem, smem], out_specs=vmem,
        compiler_params=params(16),
    )(drops, bin_blocks, bin_counts)
    received = exchange(packed)

    x_low, x_high, z_both, y_low, y_high = pl.pallas_call(
        face_kernel,
        out_shape=[shape(240), shape(240), shape(80), shape(1, 1920), shape(1, 1920)],
        in_specs=[vmem], out_specs=[vmem] * 5, compiler_params=params(16),
    )(gas)
    halo_x_low = shifted_by(x_high, "gx", 1)
    halo_x_high = shifted_by(x_low, "gx", -1)
    halo_z = shifted_by(z_both, "grp", 1)
    halo_y_low = shifted_by(y_high, "gy", 1)
    halo_y_high = shifted_by(y_low, "gy", -1)

    table = pl.pallas_call(
        table_kernel, out_shape=shape(blocks * 128, dtype=bf16), in_specs=[vmem], out_specs=vmem,
        scratch_shapes=[pltpu.VMEM((8 * plane, lanes), f32)], compiler_params=params(24),
    )(gas)

    results, owned, index = pl.pallas_call(
        sample_kernel,
        out_shape=[shape(bins * 5), shape(bins * 8), shape(peers, dtype=jnp.int32)],
        in_specs=[vmem] * 2, out_specs=[vmem] * 3,
        scratch_shapes=[
            pltpu.SMEM((peers, lanes), jnp.int32), pltpu.VMEM((64, lanes), f32), pltpu.SemaphoreType.DMA,
        ],
        compiler_params=params(24),
    )(received, table)
    returned = exchange(results)

    gas_next = pl.pallas_call(
        gas_kernel,
        out_shape=shape(5 * plane),
        in_specs=[vmem] * 2 + [smem] + [vmem] * 6, out_specs=vmem,
        scratch_shapes=[
            pltpu.VMEM((blocks * 40, lanes), f32), pltpu.VMEM((64, lanes), f32), pltpu.VMEM((320, lanes), f32),
            pltpu.VMEM((5 * plane, lanes), f32), pltpu.VMEM((5 * plane, lanes), f32),
            pltpu.VMEM((2400, lanes), f32), pltpu.VMEM((80, lanes), f32),
        ],
        compiler_params=params(32),
    )(results, owned, index, gas, halo_x_low, halo_x_high, halo_z, halo_y_low, halo_y_high)

    updated, toward_next, toward_previous = pl.pallas_call(
        leave_kernel,
        out_shape=[shape(bins * 8), shape(8, moving), shape(8, moving)],
        in_specs=[vmem, vmem, smem], out_specs=[vmem] * 3,
        scratch_shapes=[pltpu.VMEM((656, lanes), f32)], compiler_params=params(16),
    )(returned, drops, crossing)
    from_previous = shifted_by(toward_next, "gx", 1)
    from_next = shifted_by(toward_previous, "gx", -1)
    arrivals = jnp.stack([from_previous, from_next], axis=1)

    kept = pl.pallas_call(
        stay_kernel, out_shape=shape(bins * 8), in_specs=[vmem, smem, vmem], out_specs=vmem,
        compiler_params=params(16),
    )(updated, bin_counts, crossing)
    droplets_next = kept.reshape(bins, 8, lanes).transpose(1, 0, 2).reshape(8, bins * lanes)
    return gas_next.reshape(gas_state.shape), droplets_next, arrivals


def solution(mesh):
    whole = ("grp", "gx", "gy")
    in_specs = (P(None, "gx", "grp", "gy"), P(None, whole), P(whole), P(whole), P(None, whole))
    out_specs = (P(None, "gx", "grp", "gy"), P(None, whole), P(None, None, whole))
    return jax.shard_map(per_device, mesh=mesh, in_specs=in_specs, out_specs=out_specs, check_vma=False)
```

profile of v0, /device:TPU:2, one launch (start us, length us, event | category | flops | bytes accessed | tf_op | source)
XLA Modules:
  0.0 94.1 jit_solution(11885472898941927156)
XLA Ops:
  0.6 0.0 copy-start.4
  0.6 1.0 %copy-done.4 = f32[8,16384]{1,0:T(8,128)S(1)} copy-done((f32[8,16384]{1,0:T(8,128)S(1)}, f32[8,16384]{1,0:T(8,128)}, u32[]{:S(2)}) %copy-start.4) | copy-done | bytes 524312
  1.7 0.7 copy-done.9
  2.3 0.7 copy-done.11
  3.0 0.6 shard_map.76
  3.6 0.9 all_to_all.14
  4.5 11.6 %all-to-all-start = ((f32[32,33,128]{2,1,0:T(8,128)}), f32[32,33,128]{2,1,0:T(8,128)}, u32[]{:S(2)}, u32[]{:S(2)}) async-start(f32[32,33,128]{2,1,0:T(8,128)} %all_to_all.14), calls=%async_computation | async-start | bytes 1310720 | tf_op jit(solution)/shard_map/all_to_all | solution.py:346
  16.1 0.0 copy-start
  16.1 1.2 %copy-done = f32[5,8,48,128]{3,2,1,0:T(8,128)S(1)} copy-done((f32[5,8,48,128]{3,2,1,0:T(8,128)S(1)}, f32[5,8,48,128]{3,2,1,0:T(8,128)}, u32[]{:S(2)}) %copy-start) | copy-done | bytes 983064
  17.3 8.2 %shard_map.77.table = bf16[12288,128]{1,0:T(8,128)(2,1)S(1)} custom-call(f32[1920,128]{1,0:T(8,128)S(1)} %bitcast.14), custom_call_target="tpu_custom_call" | custom-call | tf_op jit(solution)/shard_map/pallas_call | solution.py:370
  25.5 10.8 %all-to-all-done = f32[32,33,128]{2,1,0:T(8,128)} async-done(((f32[32,33,128]{2,1,0:T(8,128)}), f32[32,33,128]{2,1,0:T(8,128)}, u32[]{:S(2)}, u32[]{:S(2)}) %all-to-all-start) | async-done | bytes 540704 | tf_op jit(solution)/shard_map/all_to_all | solution.py:346
  36.3 1.9 %all_to_all.16.received = f32[1056,128]{1,0:T(8,128)} reshape(f32[32,33,128]{2,1,0:T(8,128)} %all-to-all-done) | data formatting | bytes 1081344 | tf_op jit(solution)/shard_map/all_to_all | solution.py:346
  38.2 1.0 %copy-done.3 = f32[1056,128]{1,0:T(8,128)S(1)} copy-done((f32[1056,128]{1,0:T(8,128)S(1)}, f32[1056,128]{1,0:T(8,128)}, u32[]{:S(2)}) %copy-start.3) | copy-done | bytes 540696
  39.3 5.1 %shard_map.78 = (f32[640,128]{1,0:T(8,128)S(1)}, f32[1024,128]{1,0:T(8,128)S(1)}, s32[32,128]{1,0:T(8,128)S(1)}) custom-call(f32[1056,128]{1,0:T(8,128)S(1)} %copy-done.3, bf16[12288,128]{1,0:T(8,128)(2,1)S(1)} %shard_map.77.table), custom_call_target="tpu_custom_call" | custom-call | tf_op jit(solution)/shard_map/pallas_call | solution.py:375
  44.4 0.0 copy-start.6
  44.4 0.8 copy-done.6
  45.2 0.8 all_to_all.17
  46.0 5.1 %all-to-all-start.1 = ((f32[32,20,128]{2,1,0:T(8,128)}), f32[32,20,128]{2,1,0:T(8,128)S(1)}, u32[]{:S(2)}, u32[]{:S(2)}) async-start(f32[32,20,128]{2,1,0:T(8,128)} %all_to_all.17), calls=%async_computation.1 | async-start | bytes 786432 | tf_op jit(solution)/shard_map/all_to_all | solution.py:346
  51.1 1.2 %copy-done.1 = f32[5,8,48,128]{3,2,1,0:T(8,128)S(1)} copy-done((f32[5,8,48,128]{3,2,1,0:T(8,128)S(1)}, f32[5,8,48,128]{3,2,1,0:T(8,128)}, u32[]{:S(2)}) %copy-start.1) | copy-done | bytes 983064
  52.3 1.0 %shard_map.79 = (f32[240,128]{1,0:T(8,128)S(1)}, f32[240,128]{1,0:T(8,128)S(1)}, f32[80,128]{1,0:T(8,128)S(1)}, f32[1,1920]{1,0:T(1,128)S(1)}, f32[1,1920]{1,0:T(1,128)S(1)}) custom-call(f32[1920,128]{1,0:T(8,128)S(1)} %bitcast.15), custom_call_target="tpu_custom_call" | custom-call | tf_op jit(solution)/shard_map/pallas_call | solution.py:359
  53.3 1.8 %collective-permute-start = (f32[240,128]{1,0:T(8,128)S(1)}, f32[240,128]{1,0:T(8,128)S(1)}, u32[]{:S(2)}, u32[]{:S(2)}) collective-permute-start(f32[240,128]{1,0:T(8,128)S(1)} %get-tuple-element.17), channel_id=1, source_target_pairs={{0,4},{4,8},{8,12},{12,16},{16,20},{20,24},{24,28},{28,32},{32,36}... | collective-permute-start | bytes 368648 | tf_op jit(solution)/shard_map/ppermute | solution.py:342
  55.1 3.6 %collective-permute-start.1 = (f32[240,128]{1,0:T(8,128)S(1)}, f32[240,128]{1,0:T(8,128)S(1)}, u32[]{:S(2)}, u32[]{:S(2)}) collective-permute-start(f32[240,128]{1,0:T(8,128)S(1)} %get-tuple-element.18), channel_id=1, source_target_pairs={{0,124},{4,0},{8,4},{12,8},{16,12},{20,16},{24,20},{28,24},{32,28}... | collective-permute-start | bytes 368648 | tf_op jit(solution)/shard_map/ppermute | solution.py:342
  58.6 1.5 %collective-permute-start.3 = (f32[1,1920]{1,0:T(1,128)S(1)}, f32[1,1920]{1,0:T(1,128)S(1)}, u32[]{:S(2)}, u32[]{:S(2)}) collective-permute-start(f32[1,1920]{1,0:T(1,128)S(1)} %get-tuple-element.20), channel_id=1, source_target_pairs={{0,1},{1,2},{2,3},{3,0},{4,5},{5,6},{6,7},{7,4},{8,9},{9,10},{10,1... | collective-permute-start | bytes 23048 | tf_op jit(solution)/shard_map/ppermute | solution.py:342
  60.1 0.5 collective-permute-start.4
  60.7 6.2 %all-to-all-done.1 = f32[32,20,128]{2,1,0:T(8,128)S(1)} async-done(((f32[32,20,128]{2,1,0:T(8,128)}), f32[32,20,128]{2,1,0:T(8,128)S(1)}, u32[]{:S(2)}, u32[]{:S(2)}) %all-to-all-start.1) | async-done | bytes 327712 | tf_op jit(solution)/shard_map/all_to_all | solution.py:346
  66.9 3.0 %shard_map.81 = (f32[1024,128]{1,0:T(8,128)S(1)}, f32[8,256]{1,0:T(8,128)S(1)}, f32[8,256]{1,0:T(8,128)S(1)}) custom-call(f32[640,128]{1,0:T(8,128)S(1)} %all_to_all.19.returned, f32[1024,128]{1,0:T(8,128)S(1)} %bitcast.18, s32[2,256]{1,0:T(2,128)S(1)} %copy-done.8), custom_call_target="tpu_custom_call" | custom-call | tf_op jit(solution)/shard_map/pallas_call | solution.py:398
  69.9 0.1 collective-permute-start.5
  70.0 5.3 %collective-permute-start.6 = (f32[8,256]{1,0:T(8,128)S(1)}, f32[8,256]{1,0:T(8,128)S(1)}, u32[]{:S(2)}, u32[]{:S(2)}) collective-permute-start(f32[8,256]{1,0:T(8,128)S(1)} %get-tuple-element.24), channel_id=1, source_target_pairs={{0,124},{4,0},{8,4},{12,8},{16,12},{20,16},{24,20},{28,24},{32,28}... | collective-permute-start | bytes 24584 | tf_op jit(solution)/shard_map/ppermute | solution.py:342
  75.4 1.0 %copy-done.7 = f32[1024,128]{1,0:T(8,128)S(1)} copy-done((f32[1024,128]{1,0:T(8,128)S(1)}, f32[1024,128]{1,0:T(8,128)}, u32[]{:S(2)}) %copy-start.7) | copy-done | bytes 524312
  76.4 15.4 %shard_map.80 = f32[1920,128]{1,0:T(8,128)} custom-call(f32[640,128]{1,0:T(8,128)S(1)} %get-tuple-element.14.results, f32[1024,128]{1,0:T(8,128)S(1)} %copy-done.7, s32[32,128]{1,0:T(8,128)S(1)} %get-tuple-element.16.index, f32[1920,128]{1,0:T(8,128)S(1)} %bitcast.16, f32[240,128]{1,0:T(8,128)S(1)} %collective-permute-done.x_low, ...), custom_call_target="tpu_custom_call" | custom-call | tf_op jit(solution)/shard_map/pallas_call | solution.py:386
  91.8 1.6 %shard_map.82 = f32[1024,128]{1,0:T(8,128)} custom-call(f32[1024,128]{1,0:T(8,128)S(1)} %get-tuple-element.22.updated, s32[128]{0:T(128)S(1)} %copy-done.10, s32[2,256]{1,0:T(2,128)S(1)} %copy-done.8), custom_call_target="tpu_custom_call" | custom-call | tf_op jit(solution)/shard_map/pallas_call | solution.py:408
  93.5 0.6 copy.9
  (23 shorter events, 0.1 us)
Async XLA Ops:
  0.6 1.0 %copy-start.4 = (f32[8,16384]{1,0:T(8,128)S(1)}, f32[8,16384]{1,0:T(8,128)}, u32[]{:S(2)}) copy-start(f32[8,16384]{1,0:T(8,128)} %param.6) | copy-start | bytes 1572868
  1.7 0.7 copy-start.9
  2.3 0.7 copy-start.11
  4.5 31.8 %all-to-all-start = ((f32[32,33,128]{2,1,0:T(8,128)}), f32[32,33,128]{2,1,0:T(8,128)}, u32[]{:S(2)}, u32[]{:S(2)}) async-start(f32[32,33,128]{2,1,0:T(8,128)} %all_to_all.14), calls=%async_computation | async-start | bytes 1310720 | tf_op jit(solution)/shard_map/all_to_all | solution.py:346
  16.1 1.2 %copy-start = (f32[5,8,48,128]{3,2,1,0:T(8,128)S(1)}, f32[5,8,48,128]{3,2,1,0:T(8,128)}, u32[]{:S(2)}) copy-start(f32[5,8,48,128]{3,2,1,0:T(8,128)} %param.5) | copy-start | bytes 2949124
  38.2 1.0 %copy-start.3 = (f32[1056,128]{1,0:T(8,128)S(1)}, f32[1056,128]{1,0:T(8,128)}, u32[]{:S(2)}) copy-start(f32[1056,128]{1,0:T(8,128)} %all_to_all.16.received) | copy-start | bytes 1622020
  39.3 27.6 %copy-start.8 = (s32[2,256]{1,0:T(2,128)S(1)}, s32[2,256]{1,0:T(2,128)}, u32[]{:S(2)}) copy-start(s32[2,256]{1,0:T(2,128)} %crossing.3) | copy-start | bytes 6148
  44.4 0.8 copy-start.6
  45.2 21.7 %copy-start.5 = (f32[8,16384]{1,0:T(8,128)S(1)}, f32[8,16384]{1,0:T(8,128)}, u32[]{:S(2)}) copy-start(f32[8,16384]{1,0:T(8,128)} %param.6) | copy-start | bytes 1572868
  45.2 30.2 %copy-start.2 = (f32[5,8,48,128]{3,2,1,0:T(8,128)S(1)}, f32[5,8,48,128]{3,2,1,0:T(8,128)}, u32[]{:S(2)}) copy-start(f32[5,8,48,128]{3,2,1,0:T(8,128)} %param.5) | copy-start | bytes 2949124
  46.0 45.9 %copy-start.10 = (s32[128]{0:T(128)S(1)}, s32[128]{0:T(128)}, u32[]{:S(2)}) copy-start(s32[128]{0:T(128)} %counts.3) | copy-start | bytes 1540
  46.0 20.9 %all-to-all-start.1 = ((f32[32,20,128]{2,1,0:T(8,128)}), f32[32,20,128]{2,1,0:T(8,128)S(1)}, u32[]{:S(2)}, u32[]{:S(2)}) async-start(f32[32,20,128]{2,1,0:T(8,128)} %all_to_all.17), calls=%async_computation.1 | async-start | bytes 786432 | tf_op jit(solution)/shard_map/all_to_all | solution.py:346
  51.1 1.2 %copy-start.1 = (f32[5,8,48,128]{3,2,1,0:T(8,128)S(1)}, f32[5,8,48,128]{3,2,1,0:T(8,128)}, u32[]{:S(2)}) copy-start(f32[5,8,48,128]{3,2,1,0:T(8,128)} %param.5) | copy-start | bytes 2949124
  53.3 22.1 %collective-permute-start = (f32[240,128]{1,0:T(8,128)S(1)}, f32[240,128]{1,0:T(8,128)S(1)}, u32[]{:S(2)}, u32[]{:S(2)}) collective-permute-start(f32[240,128]{1,0:T(8,128)S(1)} %get-tuple-element.17), channel_id=1, source_target_pairs={{0,4},{4,8},{8,12},{12,16},{16,20},{20,24},{24,28},{28,32},{32,36}... | collective-permute-start | bytes 368648 | tf_op jit(solution)/shard_map/ppermute | solution.py:342
  55.1 20.3 %collective-permute-start.1 = (f32[240,128]{1,0:T(8,128)S(1)}, f32[240,128]{1,0:T(8,128)S(1)}, u32[]{:S(2)}, u32[]{:S(2)}) collective-permute-start(f32[240,128]{1,0:T(8,128)S(1)} %get-tuple-element.18), channel_id=1, source_target_pairs={{0,124},{4,0},{8,4},{12,8},{16,12},{20,16},{24,20},{28,24},{32,28}... | collective-permute-start | bytes 368648 | tf_op jit(solution)/shard_map/ppermute | solution.py:342
  58.6 16.7 %collective-permute-start.2 = (f32[80,128]{1,0:T(8,128)S(1)}, f32[80,128]{1,0:T(8,128)S(1)}, u32[]{:S(2)}, u32[]{:S(2)}) collective-permute-start(f32[80,128]{1,0:T(8,128)S(1)} %get-tuple-element.19), channel_id=1, source_target_pairs={{0,128},{128,0},{1,129},{129,1},{2,130},{130,2},{3,131},{131,3},{4... | collective-permute-start | bytes 122888 | tf_op jit(solution)/shard_map/ppermute | solution.py:342
  58.6 11.3 %collective-permute-start.3 = (f32[1,1920]{1,0:T(1,128)S(1)}, f32[1,1920]{1,0:T(1,128)S(1)}, u32[]{:S(2)}, u32[]{:S(2)}) collective-permute-start(f32[1,1920]{1,0:T(1,128)S(1)} %get-tuple-element.20), channel_id=1, source_target_pairs={{0,1},{1,2},{2,3},{3,0},{4,5},{5,6},{6,7},{7,4},{8,9},{9,10},{10,1... | collective-permute-start | bytes 23048 | tf_op jit(solution)/shard_map/ppermute | solution.py:342
  60.1 9.9 %collective-permute-start.4 = (f32[1,1920]{1,0:T(1,128)S(1)}, f32[1,1920]{1,0:T(1,128)S(1)}, u32[]{:S(2)}, u32[]{:S(2)}) collective-permute-start(f32[1,1920]{1,0:T(1,128)S(1)} %get-tuple-element.21), channel_id=1, source_target_pairs={{0,3},{1,0},{2,1},{3,2},{4,7},{5,4},{6,5},{7,6},{8,11},{9,8},{10,9... | collective-permute-start | bytes 23048 | tf_op jit(solution)/shard_map/ppermute | solution.py:342
  69.9 23.5 %collective-permute-start.5 = (f32[8,256]{1,0:T(8,128)S(1)}, f32[8,256]{1,0:T(8,128)S(1)}, u32[]{:S(2)}, u32[]{:S(2)}) collective-permute-start(f32[8,256]{1,0:T(8,128)S(1)} %get-tuple-element.23), channel_id=1, source_target_pairs={{0,4},{4,8},{8,12},{12,16},{16,20},{20,24},{24,28},{28,32},{32,36}... | collective-permute-start | bytes 24584 | tf_op jit(solution)/shard_map/ppermute | solution.py:342
  70.0 23.4 %collective-permute-start.6 = (f32[8,256]{1,0:T(8,128)S(1)}, f32[8,256]{1,0:T(8,128)S(1)}, u32[]{:S(2)}, u32[]{:S(2)}) collective-permute-start(f32[8,256]{1,0:T(8,128)S(1)} %get-tuple-element.24), channel_id=1, source_target_pairs={{0,124},{4,0},{8,4},{12,8},{16,12},{20,16},{24,20},{28,24},{32,28}... | collective-permute-start | bytes 24584 | tf_op jit(solution)/shard_map/ppermute | solution.py:342
  75.4 1.0 %copy-start.7 = (f32[1024,128]{1,0:T(8,128)S(1)}, f32[1024,128]{1,0:T(8,128)}, u32[]{:S(2)}) copy-start(f32[1024,128]{1,0:T(8,128)} %copy-done.6) | copy-start | bytes 1572868
where the time goes:
time: 94.6 us; the launch traced here: 94.1 us
  Pallas kernels  34.9 us (37%)
  starting transfers between devices  29.5 us (31%)
  waiting for transfers between devices  17 us (18%)
  local copies, waits for them, and re-layouts  11.8 us (12%)
    all_to_all x2, waiting for transfers between devices, exchange(): return lax.all_to_all(x, 'gx', split_axis=0, concat_axis=0, tiled=True)  17 us
    all_to_all x2, starting transfers between devices, exchange(): return lax.all_to_all(x, 'gx', split_axis=0, concat_axis=0, tiled=True)  16.7 us
    pallas_call x1, Pallas kernels, per_device(): pl.pallas_call(gas_kernel, out_shape=shape(5 * plane), in_specs=[vmem] *...  15.4 us
    ppermute x7, starting transfers between devices, shifted_by(): return lax.ppermute(x, axis, [(i, (i + by) % count) for i in range(count)])  12.8 us
    unnamed x25, local copies, waits for them, and re-layouts  8.24 us
    pallas_call x1, Pallas kernels, per_device(): pl.pallas_call(table_kernel, out_shape=shape(blocks * 128, dtype=bf16), i...  8.2 us
    pallas_call x1, Pallas kernels, per_device(): pl.pallas_call(sample_kernel, out_shape=[shape(bins * 5), shape(bins * 8)...  5.09 us
    all_to_all x4, local copies, waits for them, and re-layouts, exchange(): return lax.all_to_all(x, 'gx', split_axis=0, concat_axis=0, tiled=True)  3.6 us
  transfers between devices with their start and end apart: 9, of which 2 were waited for; matrix products, arithmetic and copies ran while one was open for 0% of the time, Pallas kernels for 31%

commit v1 on v0

v1 whole, which is shorter than its diff:
```python
import jax
import jax.numpy as jnp
from jax import lax
from jax.experimental import pallas as pl
from jax.experimental.pallas import tpu as pltpu
from jax.sharding import PartitionSpec as P

f32 = jnp.float32
bf16 = jnp.bfloat16

peers = 32
per_peer = 4
bins = 128
lanes = 128
blocks = 96
depth, across, height = 8, 48, 128
plane = depth * across
tiles_out = per_peer * 2 + 1
moving = 256
together = 16

vmem = pl.BlockSpec(memory_space=pltpu.VMEM)
smem = pl.BlockSpec(memory_space=pltpu.SMEM)
hbm = pl.BlockSpec(memory_space=pltpu.HBM)


def params(mib):
    return pltpu.CompilerParams(vmem_limit_bytes=mib * 1024 * 1024)


def lane_index(rows):
    return lax.broadcasted_iota(jnp.int32, (rows, lanes), 1)


def split(x):
    high = x.astype(bf16)
    return high, (x - high.astype(f32)).astype(bf16)


def pack_kernel(drops, ids, counts, out, held, numbers, sems):
    copies = [
        pltpu.make_async_copy(drops, held, sems.at[0]),
        pltpu.make_async_copy(ids, numbers.at[0], sems.at[1]),
        pltpu.make_async_copy(counts, numbers.at[1], sems.at[2]),
    ]
    for copy in copies:
        copy.start()
    row = lax.broadcasted_iota(jnp.int32, (4, lanes), 0)
    lane = lane_index(4)
    copies[1].wait()
    copies[2].wait()
    both = jnp.where(row == 0, numbers[0], jnp.where(row == 1, numbers[1], 0)).astype(f32)
    for p in range(peers):
        near = pltpu.roll(both, (lanes - p * per_peer) % lanes, 1) if p else both
        out[p * tiles_out + 8] = jnp.where(lane < per_peer, near, 0.0)
    copies[0].wait()
    for p in range(peers):
        for t in range(8):
            out[p * tiles_out + t] = held[p * 32 + t * 4 : p * 32 + t * 4 + 4, :]


def unpack(held, drops, index, index_smem, sem):
    total = held[8]
    for p in range(1, peers):
        total = total + pltpu.roll(held[p * tiles_out + 8], p * per_peer, 1)
    index[...] = total.astype(jnp.int32)
    copy = pltpu.make_async_copy(index, index_smem, sem)
    copy.start()
    for p in range(peers):
        for t in range(8):
            drops[p * 32 + t * 4 : p * 32 + t * 4 + 4, :] = held[p * tiles_out + t]
    copy.wait()


def face_kernel(gas, x_low, x_high, z_both, y_low, y_high):
    for v in range(5):
        x_low[v * across : (v + 1) * across, :] = gas[v * plane : v * plane + across, :]
        x_high[v * across : (v + 1) * across, :] = gas[(v + 1) * plane - across : (v + 1) * plane, :]
        z_both[v * 8 : (v + 1) * 8, :] = gas[pl.ds(v * plane, 8, stride=across), :]
        z_both[40 + v * 8 : 40 + (v + 1) * 8, :] = gas[pl.ds(v * plane + across - 1, 8, stride=across), :]
    row = lax.broadcasted_iota(jnp.int32, (8, lanes), 0)
    lane = lane_index(8)
    pick = jnp.where((row == 0) & (lane == 0) | (row == 1) & (lane == lanes - 1), 1.0, 0.0).astype(f32)
    ends = lax.dot_general(
        pick, gas[...], (((1,), (1,)), ((), ())),
        precision=lax.Precision.HIGHEST, preferred_element_type=f32,
    )
    y_low[...] = ends[0:1]
    y_high[...] = ends[1:2]


def trade_chunks(tiles, chunk):
    for bit in (1, 2, 4):
        upper = (chunk & bit) != 0
        traded = list(tiles)
        for a in range(8):
            if not a & bit:
                b = a | bit
                traded[a] = jnp.where(upper, pltpu.roll(tiles[b], bit * 8, 1), tiles[a])
                traded[b] = jnp.where(upper, tiles[b], pltpu.roll(tiles[a], lanes - bit * 8, 1))
        tiles = traded
    return tiles


def split_rows(tiles):
    first_high, first_low = split(jnp.concatenate(tiles[0:2], axis=0))
    second_high, second_low = split(jnp.concatenate(tiles[2:4], axis=0))
    last = tiles[4].astype(bf16).astype(f32)
    middle = jnp.concatenate([last, tiles[4] - last], axis=0).astype(bf16)
    return [first_high, second_high, middle, first_low, second_low]


high_rows = (0, 8, 16, 24, 32)
low_rows = (48, 56, 64, 72, 40)
block_rows = 80


def table_kernel(gas, out):
    lane = lane_index(8)
    chunk = lane >> 3
    first = lane < 64

    def strip(bz, carry):
        pairs = []
        for v in range(5):
            layers = [gas[pl.ds(v * plane + bz * 8 + j, 8, stride=across), :] for j in range(8)]
            pairs.append(trade_chunks(layers, chunk))
        for by in range(8):
            here = [pairs[v][by] for v in range(5)]
            other = [pltpu.roll(x, 64, 1) for x in here]
            near = [jnp.where(first, a, b) for a, b in zip(here, other)]
            far = [jnp.where(first, b, a) for a, b in zip(here, other)]
            for number, block in ((by, near), (by + 8, far)):
                start = (bz * 16 + number) * block_rows
                for n, part in enumerate(split_rows(block)):
                    out[pl.ds(pl.multiple_of(start + n * 16, 16), 16), :] = part
        return carry

    lax.fori_loop(0, 6, strip, 0)


def hats(tile):
    node = lax.broadcasted_iota(jnp.int32, (8, lanes), 0).astype(f32)
    return [jnp.maximum(0.0, 1.0 - jnp.abs(tile[a : a + 1] - node)) for a in range(3)]


def pair_weights(hat_z, hat_y):
    high, low = split(jnp.concatenate([hat_z[j : j + 1] * hat_y for j in range(8)], axis=0))
    return jnp.concatenate([high, low], axis=0)


def sample_kernel(received, table, results, held, drops, index, index_smem, products, sem):
    copy = pltpu.make_async_copy(received, held, sem)
    copy.start()
    copy.wait()
    unpack(held, drops, index, index_smem, sem)

    def some_bins(n, carry):
        for e in range(together):
            b = n * together + e
            hat_x, hat_z, hat_y = hats(drops[pl.ds(pl.multiple_of(b * 8, 8), 8), :])
            rows = table[pl.ds(pl.multiple_of(index_smem[0, b] * block_rows, 16), block_rows), :]
            product = jnp.dot(rows, pair_weights(hat_z, hat_y), preferred_element_type=f32)
            for v in range(5):
                h, l = high_rows[v], low_rows[v]
                products[pl.ds(pl.multiple_of(b * 40 + v * 8, 8), 8), :] = (product[h : h + 8] + product[l : l + 8]) * hat_x
        return carry

    lax.fori_loop(0, bins // together, some_bins, 0)

    def some_groups(n, carry):
        for e in range(4):
            g = n * 4 + e
            sampled = []
            for v in range(5):
                terms = [products[pl.ds(g * 320 + v * 8 + i, 8, stride=40), :] for i in range(8)]
                while len(terms) > 1:
                    terms = [a + b for a, b in zip(terms[0::2], terms[1::2])]
                sampled.append(terms[0])
            density, m1, m2, m3, energy = sampled
            v1, v2, v3, mass, heat = [drops[pl.ds(g * 64 + v, 8, stride=8), :] for v in range(3, 8)]
            inverse = 1.0 / density
            u1, u2, u3 = m1 * inverse, m2 * inverse, m3 * inverse
            gas_heat = 0.4 * (energy - 0.5 * (m1 * u1 + m2 * u2 + m3 * u3)) * inverse
            inverse_area = jnp.exp(jnp.log(mass) * (-2.0 / 3.0))
            rate = density * inverse_area * -0.8
            drag = jnp.exp(rate)
            values = [
                u1 + (v1 - u1) * drag,
                u2 + (v2 - u2) * drag,
                u3 + (v3 - u3) * drag,
                mass * jnp.exp(-0.2 * gas_heat * heat * inverse_area),
                gas_heat + (heat - gas_heat) * jnp.exp(rate * (1.0 / 1.5)),
            ]
            for v in range(5):
                results[g * 10 + v] = values[v][0:4]
                results[g * 10 + 5 + v] = values[v][4:8]
        return carry

    lax.fori_loop(0, 4, some_groups, 0)


def group_values(results, g):
    return [jnp.concatenate([results[g * 10 + v], results[g * 10 + 5 + v]], axis=0) for v in range(5)]


def primitives(s):
    inverse = 1.0 / s[0]
    u = [s[1] * inverse, s[2] * inverse, s[3] * inverse]
    pressure = 0.4 * (s[4] - 0.5 * (s[1] * u[0] + s[2] * u[1] + s[3] * u[2]))
    return u, pressure


def flux(s, u, pressure, a):
    normal = u[a]
    out = [s[1 + a]]
    for c in range(3):
        out.append(s[1 + c] * normal + pressure if c == a else s[1 + c] * normal)
    out.append((s[4] + pressure) * normal)
    return out


def deposit_kernel(results, received, out, drops, index, index_smem, sums, gains, sem):
    sums[...] = jnp.zeros(sums.shape, f32)
    unpack(received, drops, index, index_smem, sem)

    def some_groups(n, carry):
        for e in range(4):
            g = n * 4 + e
            v1, v2, v3, mass, heat = [drops[pl.ds(g * 64 + v, 8, stride=8), :] for v in range(3, 8)]
            w1, w2, w3, mass_new, heat_new = group_values(results, g)
            values = [
                mass - mass_new,
                mass * v1 - mass_new * w1,
                mass * v2 - mass_new * w2,
                mass * v3 - mass_new * w3,
                0.5 * mass * (v1 * v1 + v2 * v2 + v3 * v3) + mass * heat
                - 0.5 * mass_new * (w1 * w1 + w2 * w2 + w3 * w3) - mass_new * heat_new,
            ]
            for v in range(5):
                gains[pl.ds(g * 64 + v, 8, stride=8), :] = 4.0 * values[v]
        return carry

    lax.fori_loop(0, 4, some_groups, 0)
    lane8 = lane_index(8)

    def some_bins(n, carry):
        for e in range(together):
            b = n * together + e
            here = pl.ds(pl.multiple_of(b * 8, 8), 8)
            hat_x, hat_z, hat_y = hats(drops[here, :])
            live = jnp.where(lane8 < index_smem[1, b], gains[here, :], 0.0)
            spread = jnp.concatenate(split_rows([live[v : v + 1] * hat_x for v in range(5)]), axis=0)
            added = lax.dot_general(
                spread, pair_weights(hat_z, hat_y), (((1,), (1,)), ((), ())), preferred_element_type=f32
            )
            start = index_smem[0, b] * 40
            for v in range(5):
                h, l = high_rows[v], low_rows[v]
                place = pl.ds(pl.multiple_of(start + v * 8, 8), 8)
                sums[place, :] = sums[place, :] + (added[h : h + 8] + added[l : l + 8])
        return carry

    lax.fori_loop(0, bins // together, some_bins, 0)
    chunk = lane8 >> 3
    first = lane8 < 64

    def strip(bz, carry):
        for v in range(5):
            pairs = []
            for by in range(8):
                near = sums[pl.ds(pl.multiple_of((bz * 16 + by) * 40 + v * 8, 8), 8), :]
                far = sums[pl.ds(pl.multiple_of((bz * 16 + by + 8) * 40 + v * 8, 8), 8), :]
                pairs.append(jnp.where(first, near + pltpu.roll(near, 64, 1), far + pltpu.roll(far, 64, 1)))
            for j, layer in enumerate(trade_chunks(pairs, chunk)):
                out[pl.ds(v * plane + bz * 8 + j, 8, stride=across), :] = layer
        return carry

    lax.fori_loop(0, 6, strip, 0)


def flow_kernel(gas, sources, x_low, x_high, z_both, y_low, y_high, out, y_ends, x_padded, z_flux):
    row8 = lax.broadcasted_iota(jnp.int32, (8, lanes), 0)
    lane8 = lane_index(8)
    place = jnp.where((row8 == 0) & (lane8 == 0) | (row8 == 1) & (lane8 == lanes - 1), 1.0, 0.0).astype(f32)
    ends = jnp.concatenate([y_low[...], y_high[...], jnp.zeros((6, 5 * plane), f32)], axis=0)
    y_ends[...] = lax.dot_general(
        ends, place, (((0,), (0,)), ((), ())),
        precision=lax.Precision.HIGHEST, preferred_element_type=f32,
    )
    for v in range(5):
        x_padded[v * 480 : v * 480 + across, :] = x_low[v * across : (v + 1) * across, :]
        x_padded[v * 480 + across : v * 480 + 432, :] = gas[v * plane : (v + 1) * plane, :]
        x_padded[v * 480 + 432 : (v + 1) * 480, :] = x_high[v * across : (v + 1) * across, :]
    for side in range(2):
        edge = [z_both[side * 40 + v * 8 : side * 40 + (v + 1) * 8, :] for v in range(5)]
        edge_flux = flux(edge, *primitives(edge), 1)
        for v in range(5):
            z_flux[side * 40 + v * 8 : side * 40 + (v + 1) * 8, :] = edge_flux[v]

    row = lax.broadcasted_iota(jnp.int32, (across, lanes), 0)
    lane = lane_index(across)

    def layer(i, carry):
        def cells(at):
            return [x_padded[pl.ds(pl.multiple_of(v * 480 + at * across, 8), across), :] for v in range(5)]

        def rows(v):
            return pl.ds(pl.multiple_of(v * plane + i * across, 8), across)

        here, below, above = cells(i + 1), cells(i), cells(i + 2)
        u, pressure = primitives(here)
        flux_above = flux(above, *primitives(above), 0)
        flux_below = flux(below, *primitives(below), 0)
        flux_z = flux(here, u, pressure, 1)
        flux_y = flux(here, u, pressure, 2)
        ends = [y_ends[rows(v), :] for v in range(5)]
        flux_ends = flux(ends, *primitives(ends), 2)
        for v in range(5):
            z_low = z_both[pl.ds(40 + v * 8 + i, 1), :]
            z_high = z_both[pl.ds(v * 8 + i, 1), :]
            z_low_flux = z_flux[pl.ds(40 + v * 8 + i, 1), :]
            z_high_flux = z_flux[pl.ds(v * 8 + i, 1), :]

            def z_pair(x, low, high):
                return (
                    jnp.where(row == 0, low, pltpu.roll(x, 1, 0)),
                    jnp.where(row == across - 1, high, pltpu.roll(x, across - 1, 0)),
                )

            def y_pair(x, end):
                return (
                    jnp.where(lane == 0, end, pltpu.roll(x, 1, 1)),
                    jnp.where(lane == lanes - 1, end, pltpu.roll(x, lanes - 1, 1)),
                )

            z_down, z_up = z_pair(here[v], z_low, z_high)
            z_flux_down, z_flux_up = z_pair(flux_z[v], z_low_flux, z_high_flux)
            y_down, y_up = y_pair(here[v], ends[v])
            y_flux_down, y_flux_up = y_pair(flux_y[v], flux_ends[v])
            spread = (below[v] + above[v]) + (z_down + z_up) + (y_down + y_up) - 6.0 * here[v]
            change = (flux_above[v] - flux_below[v]) + (z_flux_up - z_flux_down) + (y_flux_up - y_flux_down)
            flow = 0.5 * change - 1.5 * spread
            out[rows(v), :] = here[v] - 0.1 * flow + sources[rows(v), :]
        return carry

    lax.fori_loop(0, depth, layer, 0)


def leave_kernel(returned, drops, crossing, updated, toward_next, toward_previous):
    for g in range(bins // 8):
        values = group_values(returned, g)
        for v in range(5):
            updated[pl.ds(g * 64 + 3 + v, 8, stride=8), :] = values[v]
        for a in range(3):
            at = pl.ds(g * 64 + a, 8, stride=8)
            updated[at, :] = drops[at, :] + 0.2 * values[a]

    lane = lane_index(8)

    def batch(s, carry):
        tiles = list(carry)
        for t in range(4):
            for e in range(8):
                target = s * 8 + e
                slot = crossing[t // 2, (t % 2) * lanes + target]
                tile = updated[pl.ds(pl.multiple_of((slot >> 7) * 8, 8), 8), :]
                moved = pltpu.roll(tile, (target - slot) & (lanes - 1), 1)
                tiles[t] = jnp.where(lane == target, moved, tiles[t])
        return tuple(tiles)

    tiles = lax.fori_loop(0, lanes // 8, batch, (jnp.zeros((8, lanes), f32),) * 4)
    toward_next[...] = jnp.concatenate(tiles[0:2], axis=1)
    toward_previous[...] = jnp.concatenate(tiles[2:4], axis=1)


def stay_kernel(updated, counts, crossing, out):
    row = lax.broadcasted_iota(jnp.int32, (bins, moving), 0)
    departed = None
    for side in range(2):
        slots = crossing[side : side + 1, :]
        in_bin = jnp.where(row == (slots >> 7), 1.0, 0.0).astype(bf16)
        in_lane = jnp.where(row == (slots & (lanes - 1)), 1.0, 0.0).astype(bf16)
        part = lax.dot_general(in_bin, in_lane, (((1,), (1,)), ((), ())), preferred_element_type=f32)
        departed = part if departed is None else departed + part
    stays = 1.0 - departed
    lane = lane_index(1)
    for b in range(bins):
        keep = jnp.where(lane < counts[b], stays[b : b + 1], 0.0)
        out[b * 8 : (b + 1) * 8, :] = updated[b * 8 : (b + 1) * 8, :] * keep


def shape(rows, columns=lanes, dtype=f32):
    return jax.ShapeDtypeStruct((rows, columns), dtype)


def shifted_by(x, axis, by):
    count = lax.axis_size(axis)
    return lax.ppermute(x, axis, [(i, (i + by) % count) for i in range(count)])


def exchange(x):
    return lax.all_to_all(x, "gx", split_axis=0, concat_axis=0, tiled=True)


def call(kernel, out_shape, in_specs, mib, scratch=()):
    one = not isinstance(out_shape, list)
    return pl.pallas_call(
        kernel, name=kernel.__name__, out_shape=out_shape, in_specs=in_specs,
        out_specs=vmem if one else [vmem] * len(out_shape),
        scratch_shapes=list(scratch), compiler_params=params(mib),
    )


def pack(drops, bin_blocks, bin_counts):
    return call(
        pack_kernel, jax.ShapeDtypeStruct((peers * tiles_out, 4, lanes), f32), [hbm] * 3, 60,
        [pltpu.VMEM((bins * 8, lanes), f32), pltpu.VMEM((2, 1, lanes), jnp.int32), pltpu.SemaphoreType.DMA((3,))],
    )(drops, bin_blocks.reshape(1, bins), bin_counts.reshape(1, bins))


def faces(gas):
    return call(face_kernel, [shape(240), shape(240), shape(80), shape(1, 1920), shape(1, 1920)], [vmem], 16)(gas)


def make_table(gas):
    return call(table_kernel, shape(blocks * block_rows, dtype=bf16), [vmem], 24)(gas)


unpack_scratch = [
    pltpu.VMEM((bins * 8, lanes), f32), pltpu.VMEM((4, lanes), jnp.int32), pltpu.SMEM((4, lanes), jnp.int32),
]


def sample(received, table):
    return call(
        sample_kernel, jax.ShapeDtypeStruct((peers * 5, 4, lanes), f32), [hbm, vmem], 24,
        [pltpu.VMEM((peers * tiles_out, 4, lanes), f32)] + unpack_scratch
        + [pltpu.VMEM((bins * 40, lanes), f32), pltpu.SemaphoreType.DMA],
    )(received, table)


def deposit(results, received):
    return call(
        deposit_kernel, shape(5 * plane), [vmem, vmem], 24,
        unpack_scratch
        + [pltpu.VMEM((blocks * 40, lanes), f32), pltpu.VMEM((bins * 8, lanes), f32), pltpu.SemaphoreType.DMA],
    )(results, received)


def advance(gas, sources, halos):
    return call(
        flow_kernel, shape(5 * plane), [vmem] * 7, 24,
        [pltpu.VMEM((5 * plane, lanes), f32), pltpu.VMEM((2400, lanes), f32), pltpu.VMEM((80, lanes), f32)],
    )(gas, sources, *halos)


def leave(returned, drops, crossing):
    return call(
        leave_kernel, [shape(bins * 8), shape(8, moving), shape(8, moving)], [vmem, vmem, smem], 16
    )(returned, drops, crossing)


def stay(updated, bin_counts, crossing):
    return call(stay_kernel, shape(bins * 8), [vmem, smem, vmem], 16)(updated, bin_counts, crossing)


def per_device(gas_state, droplets, bin_blocks, bin_counts, crossing):
    gas = gas_state.reshape(5 * plane, lanes)
    drops = droplets.reshape(8, bins, lanes).transpose(1, 0, 2).reshape(bins * 8, lanes)
    received = exchange(pack(drops, bin_blocks, bin_counts))

    x_low, x_high, z_both, y_low, y_high = faces(gas)
    halos = (
        shifted_by(x_high, "gx", 1),
        shifted_by(x_low, "gx", -1),
        shifted_by(z_both, "grp", 1),
        shifted_by(y_high, "gy", 1),
        shifted_by(y_low, "gy", -1),
    )
    table = make_table(gas)
    received, halos = lax.optimization_barrier((received, halos))
    results = sample(received, table)
    returned = exchange(results)
    gas_next = advance(gas, deposit(results, received), halos)
    returned, gas_next = lax.optimization_barrier((returned, gas_next))
    updated, toward_next, toward_previous = leave(returned, drops, crossing)
    from_previous = shifted_by(toward_next, "gx", 1)
    from_next = shifted_by(toward_previous, "gx", -1)
    arrivals = jnp.stack([from_previous, from_next], axis=1)
    kept = stay(updated, bin_counts, crossing)
    droplets_next = kept.reshape(bins, 8, lanes).transpose(1, 0, 2).reshape(8, bins * lanes)
    return gas_next.reshape(gas_state.shape), droplets_next, arrivals


def solution(mesh):
    whole = ("grp", "gx", "gy")
    in_specs = (P(None, "gx", "grp", "gy"), P(None, whole), P(whole), P(whole), P(None, whole))
    out_specs = (P(None, "gx", "grp", "gy"), P(None, whole), P(None, None, whole))
    return jax.shard_map(per_device, mesh=mesh, in_specs=in_specs, out_specs=out_specs, check_vma=False)
```

time: 94.6 us -> 70.5 us (0.75)
  the two profiles are of different devices: /device:TPU:2 before, /device:TPU:122 now
where the time goes in v1:
time: 70.5 us; the launch traced here: 70.1 us
  starting transfers between devices  25.7 us (36%)
  Pallas kernels  24.9 us (35%)
  waiting for transfers between devices  14.4 us (20%)
  local copies, waits for them, and re-layouts  4.27 us (6%)
  between operations  0.78 us (1%)
    all_to_all x2, starting transfers between devices, exchange(): return lax.all_to_all(x, 'gx', split_axis=0, concat_axis=0, tiled=True)  18.3 us
    ppermute x7, waiting for transfers between devices, shifted_by(): return lax.ppermute(x, axis, [(i, (i + by) % count) for i in range(count)])  14.4 us
    ppermute x7, starting transfers between devices, shifted_by(): return lax.ppermute(x, axis, [(i, (i + by) % count) for i in range(count)])  7.47 us
    pallas_call x1, Pallas kernels, deposit(): call(deposit_kernel, shape(5 * plane), [vmem, vmem], 24, unpack_scratch +...  7.4 us
    unnamed x25, local copies, waits for them, and re-layouts  4.27 us
    pallas_call x1, Pallas kernels, sample(): call(sample_kernel, jax.ShapeDtypeStruct((peers * 5, 4, lanes), f32), [hb...  4.04 us
    pallas_call x1, Pallas kernels, advance(): call(flow_kernel, shape(5 * plane), [vmem] * 7, 24, [pltpu.VMEM((5 * plan...  3.73 us
    pallas_call x1, Pallas kernels, leave(): call(leave_kernel, [shape(bins * 8), shape(8, moving), shape(8, moving)],...  3.03 us
  transfers between devices with their start and end apart: 9, of which 4 were waited for; matrix products, arithmetic and copies ran while one was open for 0% of the time, Pallas kernels for 23%

profile of v1, /device:TPU:122, one launch (start us, length us, event | category | flops | bytes accessed | tf_op | source)
XLA Modules:
  0.0 70.1 jit_solution(9070279396076489213)
XLA Ops:
  0.6 2.0 %pack_kernel.1 = f32[288,4,128]{2,1,0:T(4,128)} custom-call(f32[1024,128]{1,0:T(8,128)} %bitcast.19, s32[1,128]{1,0:T(1,128)} %bitcast.26, s32[1,128]{1,0:T(1,128)} %bitcast.21), custom_call_target="tpu_custom_call" | custom-call | tf_op jit(solution)/shard_map/pack_kernel/pallas_call | solution.py:416
  2.6 10.1 %all-to-all-start = ((f32[288,4,128]{2,1,0:T(4,128)}), f32[288,4,128]{2,1,0:T(4,128)S(1)}, u32[]{:S(2)}, u32[]{:S(2)}) async-start(f32[288,4,128]{2,1,0:T(4,128)} %pack_kernel.1), calls=%async_computation | async-start | bytes 1179648 | tf_op jit(solution)/shard_map/all_to_all | solution.py:403
  12.8 1.0 %face_kernel.1 = (f32[240,128]{1,0:T(8,128)S(1)}, f32[240,128]{1,0:T(8,128)S(1)}, f32[80,128]{1,0:T(8,128)S(1)}, f32[1,1920]{1,0:T(1,128)S(1)}, f32[1,1920]{1,0:T(1,128)S(1)}) custom-call(f32[1920,128]{1,0:T(8,128)S(1)} %bitcast.16), custom_call_target="tpu_custom_call" | custom-call | tf_op jit(solution)/shard_map/face_kernel/pallas_call | solution.py:423
  13.8 2.7 %collective-permute-start = (f32[240,128]{1,0:T(8,128)S(1)}, f32[240,128]{1,0:T(8,128)S(1)}, u32[]{:S(2)}, u32[]{:S(2)}) collective-permute-start(f32[240,128]{1,0:T(8,128)S(1)} %get-tuple-element.19), channel_id=1, source_target_pairs={{0,4},{4,8},{8,12},{12,16},{16,20},{20,24},{24,28},{28,32},{32,36}... | collective-permute-start | bytes 368648 | tf_op jit(solution)/shard_map/ppermute | solution.py:399
  16.4 0.0 collective-permute-start.1
  16.5 1.5 %collective-permute-start.3 = (f32[1,1920]{1,0:T(1,128)S(1)}, f32[1,1920]{1,0:T(1,128)S(1)}, u32[]{:S(2)}, u32[]{:S(2)}) collective-permute-start(f32[1,1920]{1,0:T(1,128)S(1)} %get-tuple-element.22), channel_id=1, source_target_pairs={{0,1},{1,2},{2,3},{3,0},{4,5},{5,6},{6,7},{7,4},{8,9},{9,10},{10,1... | collective-permute-start | bytes 23048 | tf_op jit(solution)/shard_map/ppermute | solution.py:399
  17.9 0.5 collective-permute-start.4
  18.5 2.1 %table_kernel.1.table = bf16[7680,128]{1,0:T(8,128)(2,1)S(1)} custom-call(f32[1920,128]{1,0:T(8,128)S(1)} %bitcast.17), custom_call_target="tpu_custom_call" | custom-call | tf_op jit(solution)/shard_map/table_kernel/pallas_call | solution.py:427
  20.6 0.0 collective-permute-done.3.y_low
  20.6 1.0 %collective-permute-done.4.y_high = f32[1,1920]{1,0:T(1,128)S(1)} collective-permute-done((f32[1,1920]{1,0:T(1,128)S(1)}, f32[1,1920]{1,0:T(1,128)S(1)}, u32[]{:S(2)}, u32[]{:S(2)}) %collective-permute-start.4) | collective-permute-done | bytes 7712 | tf_op jit(solution)/shard_map/ppermute | solution.py:399
  21.6 0.6 copy-done.8
  22.2 5.6 %collective-permute-done.x_low = f32[240,128]{1,0:T(8,128)S(1)} collective-permute-done((f32[240,128]{1,0:T(8,128)S(1)}, f32[240,128]{1,0:T(8,128)S(1)}, u32[]{:S(2)}, u32[]{:S(2)}) %collective-permute-start) | collective-permute-done | bytes 122912 | tf_op jit(solution)/shard_map/ppermute | solution.py:399
  27.8 0.6 copy-done.4
  28.5 2.5 %collective-permute-done.1.x_high = f32[240,128]{1,0:T(8,128)S(1)} collective-permute-done((f32[240,128]{1,0:T(8,128)S(1)}, f32[240,128]{1,0:T(8,128)S(1)}, u32[]{:S(2)}, u32[]{:S(2)}) %collective-permute-start.1) | collective-permute-done | bytes 122912 | tf_op jit(solution)/shard_map/ppermute | solution.py:399
  31.0 0.6 copy-done.6
  31.6 0.0 all-to-all-done.received
  31.6 4.0 %sample_kernel.1.results = f32[160,4,128]{2,1,0:T(4,128)S(1)} custom-call(f32[288,4,128]{2,1,0:T(4,128)S(1)} %all-to-all-done.received, bf16[7680,128]{1,0:T(8,128)(2,1)S(1)} %table_kernel.1.table), custom_call_target="tpu_custom_call" | custom-call | tf_op jit(solution)/shard_map/sample_kernel/pallas_call | solution.py:436
  35.6 0.0 copy-start.1
  35.7 0.7 %copy-done.1 = f32[160,4,128]{2,1,0:T(4,128)} copy-done((f32[160,4,128]{2,1,0:T(4,128)}, f32[160,4,128]{2,1,0:T(4,128)S(1)}, u32[]{:S(2)}) %copy-start.1) | copy-done | bytes 327704
  36.4 8.2 %all-to-all-start.1 = ((f32[160,4,128]{2,1,0:T(4,128)}), f32[160,4,128]{2,1,0:T(4,128)S(1)}, u32[]{:S(2)}, u32[]{:S(2)}) async-start(f32[160,4,128]{2,1,0:T(4,128)} %copy-done.1), calls=%async_computation.1 | async-start | bytes 655360 | tf_op jit(solution)/shard_map/all_to_all | solution.py:403
  44.5 0.0 copy-start.2
  44.6 1.0 %copy-done.2 = f32[160,4,128]{2,1,0:T(4,128)S(1)} copy-done((f32[160,4,128]{2,1,0:T(4,128)S(1)}, f32[160,4,128]{2,1,0:T(4,128)}, u32[]{:S(2)}) %copy-start.2) | copy-done | bytes 327704
  45.5 7.4 %deposit_kernel.1.sources = f32[1920,128]{1,0:T(8,128)S(1)} custom-call(f32[160,4,128]{2,1,0:T(4,128)S(1)} %copy-done.2, f32[288,4,128]{2,1,0:T(4,128)S(1)} %all-to-all-done.received), custom_call_target="tpu_custom_call" | custom-call | tf_op jit(solution)/shard_map/deposit_kernel/pallas_call | solution.py:444
  53.0 0.0 copy-start.3
  53.0 0.0 copy-start.10
  53.0 0.0 copy-start.11
  53.0 3.7 %flow_kernel.1 = f32[1920,128]{1,0:T(8,128)} custom-call(f32[1920,128]{1,0:T(8,128)S(1)} %bitcast.18, f32[1920,128]{1,0:T(8,128)S(1)} %deposit_kernel.1.sources, f32[240,128]{1,0:T(8,128)S(1)} %copy-done.5, f32[240,128]{1,0:T(8,128)S(1)} %copy-done.7, f32[80,128]{1,0:T(8,128)S(1)} %copy-done.9, f32[1,1920]{1,0:T(1,128)S(1)} %collective-permute-done.3.y_low, ...), custom_call_target="tpu_custom_call" | custom-call | tf_op jit(solution)/shard_map/flow_kernel/pallas_call | solution.py:452
  56.8 3.0 %leave_kernel.1 = (f32[1024,128]{1,0:T(8,128)S(1)}, f32[8,256]{1,0:T(8,128)S(1)}, f32[8,256]{1,0:T(8,128)S(1)}) custom-call(f32[160,4,128]{2,1,0:T(4,128)S(1)} %all-to-all-done.1.returned, f32[1024,128]{1,0:T(8,128)S(1)} %bitcast.20, s32[2,256]{1,0:T(2,128)S(1)} %copy-done.10), custom_call_target="tpu_custom_call" | custom-call | tf_op jit(solution)/shard_map/leave_kernel/pallas_call | solution.py:459
  59.8 2.7 %collective-permute-start.5 = (f32[8,256]{1,0:T(8,128)S(1)}, f32[8,256]{1,0:T(8,128)S(1)}, u32[]{:S(2)}, u32[]{:S(2)}) collective-permute-start(f32[8,256]{1,0:T(8,128)S(1)} %get-tuple-element.33), channel_id=1, source_target_pairs={{0,4},{4,8},{8,12},{12,16},{16,20},{20,24},{24,28},{28,32},{32,36}... | collective-permute-start | bytes 24584 | tf_op jit(solution)/shard_map/ppermute | solution.py:399
  62.5 1.6 %stay_kernel.1 = f32[1024,128]{1,0:T(8,128)} custom-call(f32[1024,128]{1,0:T(8,128)S(1)} %get-tuple-element.32.updated, s32[128]{0:T(128)S(1)} %copy-done.11, s32[2,256]{1,0:T(2,128)S(1)} %copy-done.10), custom_call_target="tpu_custom_call" | custom-call | tf_op jit(solution)/shard_map/stay_kernel/pallas_call | solution.py:465
  64.1 5.4 %collective-permute-done.6 = f32[8,256]{1,0:T(8,128)S(1)} collective-permute-done((f32[8,256]{1,0:T(8,128)S(1)}, f32[8,256]{1,0:T(8,128)S(1)}, u32[]{:S(2)}, u32[]{:S(2)}) %collective-permute-start.6) | collective-permute-done | bytes 8224 | tf_op jit(solution)/shard_map/ppermute | solution.py:399
  69.5 0.6 copy.8
  (20 shorter events, 0.0 us)
Async XLA Ops:
  0.6 12.2 %copy-start = (f32[5,8,48,128]{3,2,1,0:T(8,128)S(1)}, f32[5,8,48,128]{3,2,1,0:T(8,128)}, u32[]{:S(2)}) copy-start(f32[5,8,48,128]{3,2,1,0:T(8,128)} %param.5) | copy-start | bytes 2949124
  2.6 28.9 %all-to-all-start = ((f32[288,4,128]{2,1,0:T(4,128)}), f32[288,4,128]{2,1,0:T(4,128)S(1)}, u32[]{:S(2)}, u32[]{:S(2)}) async-start(f32[288,4,128]{2,1,0:T(4,128)} %pack_kernel.1), calls=%async_computation | async-start | bytes 1179648 | tf_op jit(solution)/shard_map/all_to_all | solution.py:403
  13.8 14.1 %collective-permute-start = (f32[240,128]{1,0:T(8,128)S(1)}, f32[240,128]{1,0:T(8,128)S(1)}, u32[]{:S(2)}, u32[]{:S(2)}) collective-permute-start(f32[240,128]{1,0:T(8,128)S(1)} %get-tuple-element.19), channel_id=1, source_target_pairs={{0,4},{4,8},{8,12},{12,16},{16,20},{20,24},{24,28},{28,32},{32,36}... | collective-permute-start | bytes 368648 | tf_op jit(solution)/shard_map/ppermute | solution.py:399
  16.4 14.5 %collective-permute-start.1 = (f32[240,128]{1,0:T(8,128)S(1)}, f32[240,128]{1,0:T(8,128)S(1)}, u32[]{:S(2)}, u32[]{:S(2)}) collective-permute-start(f32[240,128]{1,0:T(8,128)S(1)} %get-tuple-element.20), channel_id=1, source_target_pairs={{0,124},{4,0},{8,4},{12,8},{16,12},{20,16},{24,20},{28,24},{32,28}... | collective-permute-start | bytes 368648 | tf_op jit(solution)/shard_map/ppermute | solution.py:399
  16.4 5.1 %collective-permute-start.2 = (f32[80,128]{1,0:T(8,128)S(1)}, f32[80,128]{1,0:T(8,128)S(1)}, u32[]{:S(2)}, u32[]{:S(2)}) collective-permute-start(f32[80,128]{1,0:T(8,128)S(1)} %get-tuple-element.21), channel_id=1, source_target_pairs={{0,128},{128,0},{1,129},{129,1},{2,130},{130,2},{3,131},{131,3},{4... | collective-permute-start | bytes 122888 | tf_op jit(solution)/shard_map/ppermute | solution.py:399
  16.5 4.2 %collective-permute-start.3 = (f32[1,1920]{1,0:T(1,128)S(1)}, f32[1,1920]{1,0:T(1,128)S(1)}, u32[]{:S(2)}, u32[]{:S(2)}) collective-permute-start(f32[1,1920]{1,0:T(1,128)S(1)} %get-tuple-element.22), channel_id=1, source_target_pairs={{0,1},{1,2},{2,3},{3,0},{4,5},{5,6},{6,7},{7,4},{8,9},{9,10},{10,1... | collective-permute-start | bytes 23048 | tf_op jit(solution)/shard_map/ppermute | solution.py:399
  17.9 3.6 %collective-permute-start.4 = (f32[1,1920]{1,0:T(1,128)S(1)}, f32[1,1920]{1,0:T(1,128)S(1)}, u32[]{:S(2)}, u32[]{:S(2)}) collective-permute-start(f32[1,1920]{1,0:T(1,128)S(1)} %get-tuple-element.23), channel_id=1, source_target_pairs={{0,3},{1,0},{2,1},{3,2},{4,7},{5,4},{6,5},{7,6},{8,11},{9,8},{10,9... | collective-permute-start | bytes 23048 | tf_op jit(solution)/shard_map/ppermute | solution.py:399
  21.6 0.6 copy-start.8
  27.8 0.6 copy-start.4
  30.9 0.6 copy-start.6
  35.6 0.7 %copy-start.1 = (f32[160,4,128]{2,1,0:T(4,128)}, f32[160,4,128]{2,1,0:T(4,128)S(1)}, u32[]{:S(2)}) copy-start(f32[160,4,128]{2,1,0:T(4,128)S(1)} %sample_kernel.1.results) | copy-start | bytes 983044
  36.4 16.6 %copy-start.5 = (f32[240,128]{1,0:T(8,128)S(1)}, f32[240,128]{1,0:T(8,128)}, u32[]{:S(2)}) copy-start(f32[240,128]{1,0:T(8,128)} %copy-done.4) | copy-start | bytes 368644
  36.4 16.6 %copy-start.7 = (f32[240,128]{1,0:T(8,128)S(1)}, f32[240,128]{1,0:T(8,128)}, u32[]{:S(2)}) copy-start(f32[240,128]{1,0:T(8,128)} %copy-done.6) | copy-start | bytes 368644
  36.4 16.6 %copy-start.9 = (f32[80,128]{1,0:T(8,128)S(1)}, f32[80,128]{1,0:T(8,128)}, u32[]{:S(2)}) copy-start(f32[80,128]{1,0:T(8,128)} %copy-done.8) | copy-start | bytes 122884
  36.4 20.4 %all-to-all-start.1 = ((f32[160,4,128]{2,1,0:T(4,128)}), f32[160,4,128]{2,1,0:T(4,128)S(1)}, u32[]{:S(2)}, u32[]{:S(2)}) async-start(f32[160,4,128]{2,1,0:T(4,128)} %copy-done.1), calls=%async_computation.1 | async-start | bytes 655360 | tf_op jit(solution)/shard_map/all_to_all | solution.py:403
  44.5 1.0 %copy-start.2 = (f32[160,4,128]{2,1,0:T(4,128)S(1)}, f32[160,4,128]{2,1,0:T(4,128)}, u32[]{:S(2)}) copy-start(f32[160,4,128]{2,1,0:T(4,128)} %copy-done.1) | copy-start | bytes 983044
  53.0 3.8 %copy-start.3 = (f32[8,16384]{1,0:T(8,128)S(1)}, f32[8,16384]{1,0:T(8,128)}, u32[]{:S(2)}) copy-start(f32[8,16384]{1,0:T(8,128)} %param.6) | copy-start | bytes 1572868
  53.0 3.8 %copy-start.10 = (s32[2,256]{1,0:T(2,128)S(1)}, s32[2,256]{1,0:T(2,128)}, u32[]{:S(2)}) copy-start(s32[2,256]{1,0:T(2,128)} %crossing.3) | copy-start | bytes 6148
  53.0 9.5 %copy-start.11 = (s32[128]{0:T(128)S(1)}, s32[128]{0:T(128)}, u32[]{:S(2)}) copy-start(s32[128]{0:T(128)} %counts.1) | copy-start | bytes 1540
  59.8 4.3 %collective-permute-start.5 = (f32[8,256]{1,0:T(8,128)S(1)}, f32[8,256]{1,0:T(8,128)S(1)}, u32[]{:S(2)}, u32[]{:S(2)}) collective-permute-start(f32[8,256]{1,0:T(8,128)S(1)} %get-tuple-element.33), channel_id=1, source_target_pairs={{0,4},{4,8},{8,12},{12,16},{16,20},{20,24},{24,28},{28,32},{32,36}... | collective-permute-start | bytes 24584 | tf_op jit(solution)/shard_map/ppermute | solution.py:399
  62.5 7.0 %collective-permute-start.6 = (f32[8,256]{1,0:T(8,128)S(1)}, f32[8,256]{1,0:T(8,128)S(1)}, u32[]{:S(2)}, u32[]{:S(2)}) collective-permute-start(f32[8,256]{1,0:T(8,128)S(1)} %get-tuple-element.34), channel_id=1, source_target_pairs={{0,124},{4,0},{8,4},{12,8},{16,12},{20,16},{24,20},{28,24},{32,28}... | collective-permute-start | bytes 24584 | tf_op jit(solution)/shard_map/ppermute | solution.py:399

commit v2 on v1

--- a/solution.py
+++ b/solution.py
@@ -17,7 +17,9 @@
 plane = depth * across
 tiles_out = per_peer * 2 + 1
 moving = 256
-together = 16
+together = 64
+per_batch = 64
+quarters = 4
 
 vmem = pl.BlockSpec(memory_space=pltpu.VMEM)
 smem = pl.BlockSpec(memory_space=pltpu.SMEM)
@@ -72,7 +74,7 @@
     copy.wait()
 
 
-def face_kernel(gas, x_low, x_high, z_both, y_low, y_high):
+def face_kernel(gas, crossing, counts, x_low, x_high, z_both, y_low, y_high, keep):
     for v in range(5):
         x_low[v * across : (v + 1) * across, :] = gas[v * plane : v * plane + across, :]
         x_high[v * across : (v + 1) * across, :] = gas[(v + 1) * plane - across : (v + 1) * plane, :]
@@ -87,6 +89,18 @@
     )
     y_low[...] = ends[0:1]
     y_high[...] = ends[1:2]
+    row = lax.broadcasted_iota(jnp.int32, (bins, moving), 0)
+    departed = None
+    for side in range(2):
+        slots = crossing[side : side + 1, :]
+        in_bin = jnp.where(row == (slots >> 7), 1.0, 0.0).astype(bf16)
+        in_lane = jnp.where(row == (slots & (lanes - 1)), 1.0, 0.0).astype(bf16)
+        part = lax.dot_general(in_bin, in_lane, (((1,), (1,)), ((), ())), preferred_element_type=f32)
+        departed = part if departed is None else departed + part
+    lane = lane_index(bins)
+    own = lax.broadcasted_iota(jnp.int32, (bins, lanes), 0) == lane
+    count = jnp.sum(jnp.where(own, counts[...].astype(f32), 0.0), axis=1, keepdims=True)
+    keep[...] = jnp.where(lane.astype(f32) < count, 1.0 - departed, 0.0)
 
 
 def trade_chunks(tiles, chunk):
@@ -149,11 +163,8 @@
     return jnp.concatenate([high, low], axis=0)
 
 
-def sample_kernel(received, table, results, held, drops, index, index_smem, products, sem):
-    copy = pltpu.make_async_copy(received, held, sem)
-    copy.start()
-    copy.wait()
-    unpack(held, drops, index, index_smem, sem)
+def sample_kernel(received, table, results, drops, index, index_smem, products, sem):
+    unpack(received, drops, index, index_smem, sem)
 
     def some_bins(n, carry):
         for e in range(together):
@@ -347,47 +358,39 @@
     lax.fori_loop(0, depth, layer, 0)
 
 
-def leave_kernel(returned, drops, crossing, updated, toward_next, toward_previous):
+def leave_kernel(returned, drops, keep, crossing, stay, toward_next, toward_previous, updated, staying, sems):
+    copies = []
     for g in range(bins // 8):
         values = group_values(returned, g)
-        for v in range(5):
-            updated[pl.ds(g * 64 + 3 + v, 8, stride=8), :] = values[v]
-        for a in range(3):
-            at = pl.ds(g * 64 + a, 8, stride=8)
-            updated[at, :] = drops[at, :] + 0.2 * values[a]
+        places = [drops[pl.ds(g * 64 + a, 8, stride=8), :] + 0.2 * values[a] for a in range(3)]
+        mask = keep[g * 8 : (g + 1) * 8, :]
+        for n, value in enumerate(places + values):
+            at = pl.ds(g * 64 + n, 8, stride=8)
+            updated[at, :] = value
+            staying[at, :] = value * mask
+        if g % 4 == 3:
+            part = pl.ds((g - 3) * 64, 256)
+            copies.append(pltpu.make_async_copy(staying.at[part], stay.at[part], sems.at[g // 4]))
+            copies[-1].start()
 
     lane = lane_index(8)
 
     def batch(s, carry):
         tiles = list(carry)
-        for t in range(4):
-            for e in range(8):
-                target = s * 8 + e
+        for e in range(per_batch):
+            for t in range(4):
+                target = s * per_batch + e
                 slot = crossing[t // 2, (t % 2) * lanes + target]
                 tile = updated[pl.ds(pl.multiple_of((slot >> 7) * 8, 8), 8), :]
                 moved = pltpu.roll(tile, (target - slot) & (lanes - 1), 1)
                 tiles[t] = jnp.where(lane == target, moved, tiles[t])
         return tuple(tiles)
 
-    tiles = lax.fori_loop(0, lanes // 8, batch, (jnp.zeros((8, lanes), f32),) * 4)
+    tiles = lax.fori_loop(0, lanes // per_batch, batch, (jnp.zeros((8, lanes), f32),) * 4)
     toward_next[...] = jnp.concatenate(tiles[0:2], axis=1)
     toward_previous[...] = jnp.concatenate(tiles[2:4], axis=1)
-
-
-def stay_kernel(updated, counts, crossing, out):
-    row = lax.broadcasted_iota(jnp.int32, (bins, moving), 0)
-    departed = None
-    for side in range(2):
-        slots = crossing[side : side + 1, :]
-        in_bin = jnp.where(row == (slots >> 7), 1.0, 0.0).astype(bf16)
-        in_lane = jnp.where(row == (slots & (lanes - 1)), 1.0, 0.0).astype(bf16)
-        part = lax.dot_general(in_bin, in_lane, (((1,), (1,)), ((), ())), preferred_element_type=f32)
-        departed = part if departed is None else departed + part
-    stays = 1.0 - departed
-    lane = lane_index(1)
-    for b in range(bins):
-        keep = jnp.where(lane < counts[b], stays[b : b + 1], 0.0)
-        out[b * 8 : (b + 1) * 8, :] = updated[b * 8 : (b + 1) * 8, :] * keep
+    for copy in copies:
+        copy.wait()
 
 
 def shape(rows, columns=lanes, dtype=f32):
@@ -403,12 +406,12 @@
     return lax.all_to_all(x, "gx", split_axis=0, concat_axis=0, tiled=True)
 
 
-def call(kernel, out_shape, in_specs, mib, scratch=()):
-    one = not isinstance(out_shape, list)
+def call(kernel, out_shape, in_specs, mib, scratch=(), out_specs=None):
+    if out_specs is None:
+        out_specs = [vmem] * len(out_shape) if isinstance(out_shape, list) else vmem
     return pl.pallas_call(
         kernel, name=kernel.__name__, out_shape=out_shape, in_specs=in_specs,
-        out_specs=vmem if one else [vmem] * len(out_shape),
-        scratch_shapes=list(scratch), compiler_params=params(mib),
+        out_specs=out_specs, scratch_shapes=list(scratch), compiler_params=params(mib),
     )
 
 
@@ -419,8 +422,11 @@
     )(drops, bin_blocks.reshape(1, bins), bin_counts.reshape(1, bins))
 
 
-def faces(gas):
-    return call(face_kernel, [shape(240), shape(240), shape(80), shape(1, 1920), shape(1, 1920)], [vmem], 16)(gas)
+def faces(gas, crossing, bin_counts):
+    return call(
+        face_kernel,
+        [shape(240), shape(240), shape(80), shape(1, 1920), shape(1, 1920), shape(bins)], [vmem] * 3, 16,
+    )(gas, crossing, bin_counts.reshape(1, bins))
 
 
 def make_table(gas):
@@ -434,9 +440,8 @@
 
 def sample(received, table):
     return call(
-        sample_kernel, jax.ShapeDtypeStruct((peers * 5, 4, lanes), f32), [hbm, vmem], 24,
-        [pltpu.VMEM((peers * tiles_out, 4, lanes), f32)] + unpack_scratch
-        + [pltpu.VMEM((bins * 40, lanes), f32), pltpu.SemaphoreType.DMA],
+        sample_kernel, jax.ShapeDtypeStruct((peers * 5, 4, lanes), f32), [vmem] * 2, 24,
+        unpack_scratch + [pltpu.VMEM((bins * 40, lanes), f32), pltpu.SemaphoreType.DMA],
     )(received, table)
 
 
@@ -455,14 +460,12 @@
     )(gas, sources, *halos)
 
 
-def leave(returned, drops, crossing):
+def leave(returned, drops, keep, crossing):
     return call(
-        leave_kernel, [shape(bins * 8), shape(8, moving), shape(8, moving)], [vmem, vmem, smem], 16
-    )(returned, drops, crossing)
-
-
-def stay(updated, bin_counts, crossing):
-    return call(stay_kernel, shape(bins * 8), [vmem, smem, vmem], 16)(updated, bin_counts, crossing)
+        leave_kernel, [shape(bins * 8), shape(8, moving), shape(8, moving)], [vmem] * 3 + [smem], 16,
+        [pltpu.VMEM((bins * 8, lanes), f32), pltpu.VMEM((bins * 8, lanes), f32), pltpu.SemaphoreType.DMA((4,))],
+        [hbm, vmem, vmem],
+    )(returned, drops, keep, crossing)
 
 
 def per_device(gas_state, droplets, bin_blocks, bin_counts, crossing):
@@ -470,7 +473,7 @@
     drops = droplets.reshape(8, bins, lanes).transpose(1, 0, 2).reshape(bins * 8, lanes)
     received = exchange(pack(drops, bin_blocks, bin_counts))
 
-    x_low, x_high, z_both, y_low, y_high = faces(gas)
+    x_low, x_high, z_both, y_low, y_high, keep = faces(gas, crossing, bin_counts)
     halos = (
         shifted_by(x_high, "gx", 1),
         shifted_by(x_low, "gx", -1),
@@ -479,16 +482,17 @@
         shifted_by(y_low, "gy", -1),
     )
     table = make_table(gas)
-    received, halos = lax.optimization_barrier((received, halos))
+    received, halos_z, halos_y1, halos_y2 = lax.optimization_barrier((received,) + halos[2:])
     results = sample(received, table)
+    results, halo_x1, halo_x2 = lax.optimization_barrier((results,) + halos[:2])
+    halos = (halo_x1, halo_x2, halos_z, halos_y1, halos_y2)
     returned = exchange(results)
     gas_next = advance(gas, deposit(results, received), halos)
     returned, gas_next = lax.optimization_barrier((returned, gas_next))
-    updated, toward_next, toward_previous = leave(returned, drops, crossing)
+    kept, toward_next, toward_previous = leave(returned, drops, keep, crossing)
     from_previous = shifted_by(toward_next, "gx", 1)
     from_next = shifted_by(toward_previous, "gx", -1)
     arrivals = jnp.stack([from_previous, from_next], axis=1)
-    kept = stay(updated, bin_counts, crossing)
     droplets_next = kept.reshape(bins, 8, lanes).transpose(1, 0, 2).reshape(8, bins * lanes)
     return gas_next.reshape(gas_state.shape), droplets_next, arrivals
 

time: 70.5 us -> 66.7 us (0.946)
  Pallas kernels: 24.9 us -> 22.3 us
  waiting for transfers between devices: 14.4 us -> 12.3 us
  starting transfers between devices: 25.7 us -> 26.7 us
    ppermute x7, waiting for transfers between devices: 14.4 us -> 7.94 us  [shifted_by(): return lax.ppermute(x, axis, [(i, (i + by) % count) for i in range(count)])]
    all_to_all x2, waiting for transfers between devices: 0.01 us -> 4.38 us  [exchange(): return lax.all_to_all(x, 'gx', split_axis=0, concat_axis=0, tiled=True)]
    pallas_call x2 -> x1, Pallas kernels: 5.63 us -> 2.89 us  [sample(): call(sample_kernel, jax.ShapeDtypeStruct((peers * 5, 4, lanes), f32), [vm...]
    pallas_call x1, Pallas kernels: 3.73 us -> 4.91 us  [advance(): call(flow_kernel, shape(5 * plane), [vmem] * 7, 24, [pltpu.VMEM((5 * plan...]
    all_to_all x2, starting transfers between devices: 18.3 us -> 19.2 us  [exchange(): return lax.all_to_all(x, 'gx', split_axis=0, concat_axis=0, tiled=True)]
    pallas_call x1, Pallas kernels: 7.4 us -> 6.54 us  [deposit(): call(deposit_kernel, shape(5 * plane), [vmem, vmem], 24, unpack_scratch +...]
    pallas_call x1, Pallas kernels: 3.03 us -> 2.24 us  [leave(): call(leave_kernel, [shape(bins * 8), shape(8, moving), shape(8, moving)],...]
  transfers between devices with their start and end apart: 9 -> 9, of which waited for: 4 -> 4; matrix products, arithmetic and copies ran while one was open for 0% -> 0% of each run, Pallas kernels for 23% -> 27%
where the time goes in v2:
time: 66.7 us; the launch traced here: 66.3 us
  starting transfers between devices  26.7 us (40%)
  Pallas kernels  22.3 us (33%)
  waiting for transfers between devices  12.3 us (18%)
  local copies, waits for them, and re-layouts  4.22 us (6%)
  between operations  0.81 us (1%)
    all_to_all x2, starting transfers between devices, exchange(): return lax.all_to_all(x, 'gx', split_axis=0, concat_axis=0, tiled=True)  19.2 us
    ppermute x7, waiting for transfers between devices, shifted_by(): return lax.ppermute(x, axis, [(i, (i + by) % count) for i in range(count)])  7.94 us
    ppermute x7, starting transfers between devices, shifted_by(): return lax.ppermute(x, axis, [(i, (i + by) % count) for i in range(count)])  7.46 us
    pallas_call x1, Pallas kernels, deposit(): call(deposit_kernel, shape(5 * plane), [vmem, vmem], 24, unpack_scratch +...  6.54 us
    pallas_call x1, Pallas kernels, advance(): call(flow_kernel, shape(5 * plane), [vmem] * 7, 24, [pltpu.VMEM((5 * plan...  4.91 us
    all_to_all x2, waiting for transfers between devices, exchange(): return lax.all_to_all(x, 'gx', split_axis=0, concat_axis=0, tiled=True)  4.38 us
    unnamed x25, local copies, waits for them, and re-layouts  4.22 us
    pallas_call x1, Pallas kernels, sample(): call(sample_kernel, jax.ShapeDtypeStruct((peers * 5, 4, lanes), f32), [vm...  2.89 us
  transfers between devices with their start and end apart: 9, of which 4 were waited for; matrix products, arithmetic and copies ran while one was open for 0% of the time, Pallas kernels for 27%

profile of v2, /device:TPU:122, one launch (start us, length us, event | category | flops | bytes accessed | tf_op | source)
XLA Modules:
  0.0 66.3 jit_solution(14827421686677238035)
XLA Ops:
  0.7 2.0 %pack_kernel.1 = f32[288,4,128]{2,1,0:T(4,128)} custom-call(f32[1024,128]{1,0:T(8,128)} %bitcast.19, s32[1,128]{1,0:T(1,128)} %bitcast.26, s32[1,128]{1,0:T(1,128)} %bitcast.21), custom_call_target="tpu_custom_call" | custom-call | tf_op jit(solution)/shard_map/pack_kernel/pallas_call | solution.py:419
  2.7 10.1 %all-to-all-start = ((f32[288,4,128]{2,1,0:T(4,128)}), f32[288,4,128]{2,1,0:T(4,128)S(1)}, u32[]{:S(2)}, u32[]{:S(2)}) async-start(f32[288,4,128]{2,1,0:T(4,128)} %pack_kernel.1), calls=%async_computation | async-start | bytes 1179648 | tf_op jit(solution)/shard_map/all_to_all | solution.py:406
  12.8 1.6 %face_kernel.1 = (f32[240,128]{1,0:T(8,128)}, f32[240,128]{1,0:T(8,128)}, f32[80,128]{1,0:T(8,128)S(1)}, f32[1,1920]{1,0:T(1,128)S(1)}, f32[1,1920]{1,0:T(1,128)S(1)}, /*index=5*/f32[128,128]{1,0:T(8,128)S(1)}) custom-call(f32[1920,128]{1,0:T(8,128)S(1)} %bitcast.16, s32[2,256]{1,0:T(2,128)S(1)} %copy-done.8, s32[1,128]{1,0:T(1,128)S(1)} %bitcast.22), custom_call_target="tpu_custom_call" | custom-call | tf_op jit(solution)/shard_map/face_kernel/pallas_call | solution.py:426
  14.4 0.6 copy-done.4
  15.1 2.7 %collective-permute-start.3 = (f32[240,128]{1,0:T(8,128)}, f32[240,128]{1,0:T(8,128)}, u32[]{:S(2)}, u32[]{:S(2)}) collective-permute-start(f32[240,128]{1,0:T(8,128)} %get-tuple-element.25), channel_id=1, source_target_pairs={{0,4},{4,8},{8,12},{12,16},{16,20},{20,24},{24,28},{28,32},{32,36}... | collective-permute-start | bytes 368648 | tf_op jit(solution)/shard_map/ppermute | solution.py:402
  17.7 0.0 collective-permute-start
  17.7 1.5 %collective-permute-start.1 = (f32[1,1920]{1,0:T(1,128)S(1)}, f32[1,1920]{1,0:T(1,128)S(1)}, u32[]{:S(2)}, u32[]{:S(2)}) collective-permute-start(f32[1,1920]{1,0:T(1,128)S(1)} %get-tuple-element.22), channel_id=1, source_target_pairs={{0,1},{1,2},{2,3},{3,0},{4,5},{5,6},{6,7},{7,4},{8,9},{9,10},{10,1... | collective-permute-start | bytes 23048 | tf_op jit(solution)/shard_map/ppermute | solution.py:402
  19.2 0.5 collective-permute-start.2
  19.8 2.1 %table_kernel.1.table = bf16[7680,128]{1,0:T(8,128)(2,1)S(1)} custom-call(f32[1920,128]{1,0:T(8,128)S(1)} %bitcast.17), custom_call_target="tpu_custom_call" | custom-call | tf_op jit(solution)/shard_map/table_kernel/pallas_call | solution.py:433
  21.9 1.0 %collective-permute-done.2.y_high = f32[1,1920]{1,0:T(1,128)S(1)} collective-permute-done((f32[1,1920]{1,0:T(1,128)S(1)}, f32[1,1920]{1,0:T(1,128)S(1)}, u32[]{:S(2)}, u32[]{:S(2)}) %collective-permute-start.2) | collective-permute-done | bytes 7712 | tf_op jit(solution)/shard_map/ppermute | solution.py:402
  22.9 0.6 copy-done.9
  23.5 0.0 collective-permute-done.z_both
  23.5 0.6 copy-done.6
  24.1 4.4 %all-to-all-done.received = f32[288,4,128]{2,1,0:T(4,128)S(1)} async-done(((f32[288,4,128]{2,1,0:T(4,128)}), f32[288,4,128]{2,1,0:T(4,128)S(1)}, u32[]{:S(2)}, u32[]{:S(2)}) %all-to-all-start) | async-done | bytes 589856 | tf_op jit(solution)/shard_map/all_to_all | solution.py:406
  28.5 2.9 %sample_kernel.1.results = f32[160,4,128]{2,1,0:T(4,128)S(1)} custom-call(f32[288,4,128]{2,1,0:T(4,128)S(1)} %all-to-all-done.received, bf16[7680,128]{1,0:T(8,128)(2,1)S(1)} %table_kernel.1.table), custom_call_target="tpu_custom_call" | custom-call | tf_op jit(solution)/shard_map/sample_kernel/pallas_call | solution.py:442
  31.4 0.0 copy-start.1
  31.4 0.7 %copy-done.1 = f32[160,4,128]{2,1,0:T(4,128)} copy-done((f32[160,4,128]{2,1,0:T(4,128)}, f32[160,4,128]{2,1,0:T(4,128)S(1)}, u32[]{:S(2)}) %copy-start.1) | copy-done | bytes 327704
  32.1 0.0 collective-permute-done.3.x_low
  32.1 0.0 collective-permute-done.4.x_high
  32.1 9.1 %all-to-all-start.1 = ((f32[160,4,128]{2,1,0:T(4,128)}), f32[160,4,128]{2,1,0:T(4,128)S(1)}, u32[]{:S(2)}, u32[]{:S(2)}) async-start(f32[160,4,128]{2,1,0:T(4,128)} %copy-done.1), calls=%async_computation.1 | async-start | bytes 655360 | tf_op jit(solution)/shard_map/all_to_all | solution.py:406
  41.2 0.0 copy-start.2
  41.2 1.0 %copy-done.2 = f32[160,4,128]{2,1,0:T(4,128)S(1)} copy-done((f32[160,4,128]{2,1,0:T(4,128)S(1)}, f32[160,4,128]{2,1,0:T(4,128)}, u32[]{:S(2)}) %copy-start.2) | copy-done | bytes 327704
  42.2 6.5 %deposit_kernel.1.sources = f32[1920,128]{1,0:T(8,128)S(1)} custom-call(f32[160,4,128]{2,1,0:T(4,128)S(1)} %copy-done.2, f32[288,4,128]{2,1,0:T(4,128)S(1)} %all-to-all-done.received), custom_call_target="tpu_custom_call" | custom-call | tf_op jit(solution)/shard_map/deposit_kernel/pallas_call | solution.py:449
  48.8 0.0 copy-start.3
  48.8 4.9 %flow_kernel.1 = f32[1920,128]{1,0:T(8,128)} custom-call(f32[1920,128]{1,0:T(8,128)S(1)} %bitcast.18, f32[1920,128]{1,0:T(8,128)S(1)} %deposit_kernel.1.sources, f32[240,128]{1,0:T(8,128)} %collective-permute-done.3.x_low, f32[240,128]{1,0:T(8,128)} %collective-permute-done.4.x_high, f32[80,128]{1,0:T(8,128)S(1)} %copy-done.7, ...), custom_call_target="tpu_custom_call" | custom-call | tf_op jit(solution)/shard_map/flow_kernel/pallas_call | solution.py:457
  53.7 0.0 all-to-all-done.1.returned
  53.8 2.2 %leave_kernel.1 = (f32[1024,128]{1,0:T(8,128)}, f32[8,256]{1,0:T(8,128)S(1)}, f32[8,256]{1,0:T(8,128)S(1)}) custom-call(f32[160,4,128]{2,1,0:T(4,128)S(1)} %all-to-all-done.1.returned, f32[1024,128]{1,0:T(8,128)S(1)} %bitcast.20, f32[128,128]{1,0:T(8,128)S(1)} %copy-done.5, s32[2,256]{1,0:T(2,128)S(1)} %copy-done.8), custom_call_target="tpu_custom_call" | custom-call | tf_op jit(solution)/shard_map/leave_kernel/pallas_call | solution.py:464
  56.0 2.8 %collective-permute-start.5 = (f32[8,256]{1,0:T(8,128)S(1)}, f32[8,256]{1,0:T(8,128)S(1)}, u32[]{:S(2)}, u32[]{:S(2)}) collective-permute-start(f32[8,256]{1,0:T(8,128)S(1)} %get-tuple-element.37), channel_id=1, source_target_pairs={{0,4},{4,8},{8,12},{12,16},{16,20},{20,24},{24,28},{28,32},{32,36}... | collective-permute-start | bytes 24584 | tf_op jit(solution)/shard_map/ppermute | solution.py:402
  58.7 0.0 collective-permute-start.6
  58.8 1.4 %collective-permute-done.5 = f32[8,256]{1,0:T(8,128)S(1)} collective-permute-done((f32[8,256]{1,0:T(8,128)S(1)}, f32[8,256]{1,0:T(8,128)S(1)}, u32[]{:S(2)}, u32[]{:S(2)}) %collective-permute-start.5) | collective-permute-done | bytes 8224 | tf_op jit(solution)/shard_map/ppermute | solution.py:402
  60.1 5.6 %collective-permute-done.6 = f32[8,256]{1,0:T(8,128)S(1)} collective-permute-done((f32[8,256]{1,0:T(8,128)S(1)}, f32[8,256]{1,0:T(8,128)S(1)}, u32[]{:S(2)}, u32[]{:S(2)}) %collective-permute-start.6) | collective-permute-done | bytes 8224 | tf_op jit(solution)/shard_map/ppermute | solution.py:402
  65.7 0.6 copy.8
  (19 shorter events, 0.0 us)
Async XLA Ops:
  0.6 12.2 %copy-start.11 = (s32[128]{0:T(128)S(1)}, s32[128]{0:T(128)}, u32[]{:S(2)}) copy-start(s32[128]{0:T(128)} %param.8) | copy-start | bytes 1540
  0.6 12.2 %copy-start.8 = (s32[2,256]{1,0:T(2,128)S(1)}, s32[2,256]{1,0:T(2,128)}, u32[]{:S(2)}) copy-start(s32[2,256]{1,0:T(2,128)} %crossing.3) | copy-start | bytes 6148
  0.7 12.2 %copy-start = (f32[5,8,48,128]{3,2,1,0:T(8,128)S(1)}, f32[5,8,48,128]{3,2,1,0:T(8,128)}, u32[]{:S(2)}) copy-start(f32[5,8,48,128]{3,2,1,0:T(8,128)} %param.5) | copy-start | bytes 2949124
  2.7 25.8 %all-to-all-start = ((f32[288,4,128]{2,1,0:T(4,128)}), f32[288,4,128]{2,1,0:T(4,128)S(1)}, u32[]{:S(2)}, u32[]{:S(2)}) async-start(f32[288,4,128]{2,1,0:T(4,128)} %pack_kernel.1), calls=%async_computation | async-start | bytes 1179648 | tf_op jit(solution)/shard_map/all_to_all | solution.py:406
  14.4 0.6 copy-start.4
  15.1 17.1 %collective-permute-start.3 = (f32[240,128]{1,0:T(8,128)}, f32[240,128]{1,0:T(8,128)}, u32[]{:S(2)}, u32[]{:S(2)}) collective-permute-start(f32[240,128]{1,0:T(8,128)} %get-tuple-element.25), channel_id=1, source_target_pairs={{0,4},{4,8},{8,12},{12,16},{16,20},{20,24},{24,28},{28,32},{32,36}... | collective-permute-start | bytes 368648 | tf_op jit(solution)/shard_map/ppermute | solution.py:402
  17.7 14.4 %collective-permute-start.4 = (f32[240,128]{1,0:T(8,128)}, f32[240,128]{1,0:T(8,128)}, u32[]{:S(2)}, u32[]{:S(2)}) collective-permute-start(f32[240,128]{1,0:T(8,128)} %get-tuple-element.26), channel_id=1, source_target_pairs={{0,124},{4,0},{8,4},{12,8},{16,12},{20,16},{24,20},{28,24},{32,28}... | collective-permute-start | bytes 368648 | tf_op jit(solution)/shard_map/ppermute | solution.py:402
  17.7 5.7 %collective-permute-start = (f32[80,128]{1,0:T(8,128)S(1)}, f32[80,128]{1,0:T(8,128)S(1)}, u32[]{:S(2)}, u32[]{:S(2)}) collective-permute-start(f32[80,128]{1,0:T(8,128)S(1)} %get-tuple-element.21), channel_id=1, source_target_pairs={{0,128},{128,0},{1,129},{129,1},{2,130},{130,2},{3,131},{131,3},{4... | collective-permute-start | bytes 122888 | tf_op jit(solution)/shard_map/ppermute | solution.py:402
  17.7 4.2 %collective-permute-start.1 = (f32[1,1920]{1,0:T(1,128)S(1)}, f32[1,1920]{1,0:T(1,128)S(1)}, u32[]{:S(2)}, u32[]{:S(2)}) collective-permute-start(f32[1,1920]{1,0:T(1,128)S(1)} %get-tuple-element.22), channel_id=1, source_target_pairs={{0,1},{1,2},{2,3},{3,0},{4,5},{5,6},{6,7},{7,4},{8,9},{9,10},{10,1... | collective-permute-start | bytes 23048 | tf_op jit(solution)/shard_map/ppermute | solution.py:402
  19.2 3.6 %collective-permute-start.2 = (f32[1,1920]{1,0:T(1,128)S(1)}, f32[1,1920]{1,0:T(1,128)S(1)}, u32[]{:S(2)}, u32[]{:S(2)}) collective-permute-start(f32[1,1920]{1,0:T(1,128)S(1)} %get-tuple-element.23), channel_id=1, source_target_pairs={{0,3},{1,0},{2,1},{3,2},{4,7},{5,4},{6,5},{7,6},{8,11},{9,8},{10,9... | collective-permute-start | bytes 23048 | tf_op jit(solution)/shard_map/ppermute | solution.py:402
  22.9 0.6 copy-start.9
  23.5 0.6 copy-start.6
  31.4 0.7 %copy-start.1 = (f32[160,4,128]{2,1,0:T(4,128)}, f32[160,4,128]{2,1,0:T(4,128)S(1)}, u32[]{:S(2)}) copy-start(f32[160,4,128]{2,1,0:T(4,128)S(1)} %sample_kernel.1.results) | copy-start | bytes 983044
  32.1 16.7 %copy-start.7 = (f32[80,128]{1,0:T(8,128)S(1)}, f32[80,128]{1,0:T(8,128)}, u32[]{:S(2)}) copy-start(f32[80,128]{1,0:T(8,128)} %copy-done.6) | copy-start | bytes 122884
  32.1 16.7 %copy-start.10 = (f32[1,1920]{1,0:T(1,128)S(1)}, f32[1,1920]{1,0:T(1,128)}, u32[]{:S(2)}) copy-start(f32[1,1920]{1,0:T(1,128)} %copy-done.9) | copy-start | bytes 23044
  32.1 21.6 %all-to-all-start.1 = ((f32[160,4,128]{2,1,0:T(4,128)}), f32[160,4,128]{2,1,0:T(4,128)S(1)}, u32[]{:S(2)}, u32[]{:S(2)}) async-start(f32[160,4,128]{2,1,0:T(4,128)} %copy-done.1), calls=%async_computation.1 | async-start | bytes 655360 | tf_op jit(solution)/shard_map/all_to_all | solution.py:406
  41.2 1.0 %copy-start.2 = (f32[160,4,128]{2,1,0:T(4,128)S(1)}, f32[160,4,128]{2,1,0:T(4,128)}, u32[]{:S(2)}) copy-start(f32[160,4,128]{2,1,0:T(4,128)} %copy-done.1) | copy-start | bytes 983044
  48.8 4.9 %copy-start.3 = (f32[8,16384]{1,0:T(8,128)S(1)}, f32[8,16384]{1,0:T(8,128)}, u32[]{:S(2)}) copy-start(f32[8,16384]{1,0:T(8,128)} %param.6) | copy-start | bytes 1572868
  48.8 4.9 %copy-start.5 = (f32[128,128]{1,0:T(8,128)S(1)}, f32[128,128]{1,0:T(8,128)}, u32[]{:S(2)}) copy-start(f32[128,128]{1,0:T(8,128)} %copy-done.4) | copy-start | bytes 196612
  56.0 4.1 %collective-permute-start.5 = (f32[8,256]{1,0:T(8,128)S(1)}, f32[8,256]{1,0:T(8,128)S(1)}, u32[]{:S(2)}, u32[]{:S(2)}) collective-permute-start(f32[8,256]{1,0:T(8,128)S(1)} %get-tuple-element.37), channel_id=1, source_target_pairs={{0,4},{4,8},{8,12},{12,16},{16,20},{20,24},{24,28},{28,32},{32,36}... | collective-permute-start | bytes 24584 | tf_op jit(solution)/shard_map/ppermute | solution.py:402
  58.7 7.0 %collective-permute-start.6 = (f32[8,256]{1,0:T(8,128)S(1)}, f32[8,256]{1,0:T(8,128)S(1)}, u32[]{:S(2)}, u32[]{:S(2)}) collective-permute-start(f32[8,256]{1,0:T(8,128)S(1)} %get-tuple-element.38), channel_id=1, source_target_pairs={{0,124},{4,0},{8,4},{12,8},{16,12},{20,16},{24,20},{28,24},{32,28}... | collective-permute-start | bytes 24584 | tf_op jit(solution)/shard_map/ppermute | solution.py:402

commit v3 on v2

--- a/solution.py
+++ b/solution.py
@@ -71,7 +71,7 @@
     for p in range(peers):
         for t in range(8):
             drops[p * 32 + t * 4 : p * 32 + t * 4 + 4, :] = held[p * tiles_out + t]
-    copy.wait()
+    return copy
 
 
 def face_kernel(gas, crossing, counts, x_low, x_high, z_both, y_low, y_high, keep):
@@ -163,25 +163,19 @@
     return jnp.concatenate([high, low], axis=0)
 
 
-def sample_kernel(received, table, results, drops, index, index_smem, products, sem):
-    unpack(received, drops, index, index_smem, sem)
-
-    def some_bins(n, carry):
-        for e in range(together):
-            b = n * together + e
-            hat_x, hat_z, hat_y = hats(drops[pl.ds(pl.multiple_of(b * 8, 8), 8), :])
+def sample_kernel(received, table, results, drops, index, index_smem, products, answers, sems):
+    unpack(received, drops, index, index_smem, sems.at[quarters]).wait()
+    stores = []
+    for n in range(quarters):
+        for b in range(n * 32, n * 32 + 32):
+            hat_x, hat_z, hat_y = hats(drops[b * 8 : b * 8 + 8, :])
             rows = table[pl.ds(pl.multiple_of(index_smem[0, b] * block_rows, 16), block_rows), :]
             product = jnp.dot(rows, pair_weights(hat_z, hat_y), preferred_element_type=f32)
             for v in range(5):
                 h, l = high_rows[v], low_rows[v]
-                products[pl.ds(pl.multiple_of(b * 40 + v * 8, 8), 8), :] = (product[h : h + 8] + product[l : l + 8]) * hat_x
-        return carry
-
-    lax.fori_loop(0, bins // together, some_bins, 0)
-
-    def some_groups(n, carry):
-        for e in range(4):
-            g = n * 4 + e
+                at = b * 40 + v * 8
+                products[at : at + 8, :] = (product[h : h + 8] + product[l : l + 8]) * hat_x
+        for g in range(n * 4, n * 4 + 4):
             sampled = []
             for v in range(5):
                 terms = [products[pl.ds(g * 320 + v * 8 + i, 8, stride=40), :] for i in range(8)]
@@ -204,11 +198,13 @@
                 gas_heat + (heat - gas_heat) * jnp.exp(rate * (1.0 / 1.5)),
             ]
             for v in range(5):
-                results[g * 10 + v] = values[v][0:4]
-                results[g * 10 + 5 + v] = values[v][4:8]
-        return carry
-
-    lax.fori_loop(0, 4, some_groups, 0)
+                answers[g * 10 + v] = values[v][0:4]
+                answers[g * 10 + 5 + v] = values[v][4:8]
+        part = pl.ds(n * 40, 40)
+        stores.append(pltpu.make_async_copy(answers.at[part], results.at[part], sems.at[n]))
+        stores[n].start()
+    for copy in stores:
+        copy.wait()
 
 
 def group_values(results, g):
@@ -231,15 +227,18 @@
     return out
 
 
-def deposit_kernel(results, received, out, drops, index, index_smem, sums, gains, sem):
+def deposit_kernel(results, received, out, answers, drops, index, index_smem, sums, gains, sems):
+    load = pltpu.make_async_copy(results, answers, sems.at[1])
+    load.start()
+    copy = unpack(received, drops, index, index_smem, sems.at[0])
     sums[...] = jnp.zeros(sums.shape, f32)
-    unpack(received, drops, index, index_smem, sem)
+    load.wait()
 
     def some_groups(n, carry):
         for e in range(4):
             g = n * 4 + e
             v1, v2, v3, mass, heat = [drops[pl.ds(g * 64 + v, 8, stride=8), :] for v in range(3, 8)]
-            w1, w2, w3, mass_new, heat_new = group_values(results, g)
+            w1, w2, w3, mass_new, heat_new = group_values(answers, g)
             values = [
                 mass - mass_new,
                 mass * v1 - mass_new * w1,
@@ -253,6 +252,7 @@
         return carry
 
     lax.fori_loop(0, 4, some_groups, 0)
+    copy.wait()
     lane8 = lane_index(8)
 
     def some_bins(n, carry):
@@ -358,20 +358,15 @@
     lax.fori_loop(0, depth, layer, 0)
 
 
-def leave_kernel(returned, drops, keep, crossing, stay, toward_next, toward_previous, updated, staying, sems):
-    copies = []
+def leave_kernel(returned, drops, crossing, updated, toward_next, toward_previous, slots, sem):
+    copy = pltpu.make_async_copy(crossing, slots, sem)
+    copy.start()
     for g in range(bins // 8):
         values = group_values(returned, g)
         places = [drops[pl.ds(g * 64 + a, 8, stride=8), :] + 0.2 * values[a] for a in range(3)]
-        mask = keep[g * 8 : (g + 1) * 8, :]
         for n, value in enumerate(places + values):
-            at = pl.ds(g * 64 + n, 8, stride=8)
-            updated[at, :] = value
-            staying[at, :] = value * mask
-        if g % 4 == 3:
-            part = pl.ds((g - 3) * 64, 256)
-            copies.append(pltpu.make_async_copy(staying.at[part], stay.at[part], sems.at[g // 4]))
-            copies[-1].start()
+            updated[pl.ds(g * 64 + n, 8, stride=8), :] = value
+    copy.wait()
 
     lane = lane_index(8)
 
@@ -380,7 +375,7 @@
         for e in range(per_batch):
             for t in range(4):
                 target = s * per_batch + e
-                slot = crossing[t // 2, (t % 2) * lanes + target]
+                slot = slots[t // 2, (t % 2) * lanes + target]
                 tile = updated[pl.ds(pl.multiple_of((slot >> 7) * 8, 8), 8), :]
                 moved = pltpu.roll(tile, (target - slot) & (lanes - 1), 1)
                 tiles[t] = jnp.where(lane == target, moved, tiles[t])
@@ -389,6 +384,16 @@
     tiles = lax.fori_loop(0, lanes // per_batch, batch, (jnp.zeros((8, lanes), f32),) * 4)
     toward_next[...] = jnp.concatenate(tiles[0:2], axis=1)
     toward_previous[...] = jnp.concatenate(tiles[2:4], axis=1)
+
+
+def stay_kernel(updated, keep, out, staying, sems):
+    copies = []
+    for n in range(quarters):
+        for b in range(n * 32, n * 32 + 32):
+            staying[b * 8 : (b + 1) * 8, :] = updated[b * 8 : (b + 1) * 8, :] * keep[b : b + 1, :]
+        part = pl.ds(n * 256, 256)
+        copies.append(pltpu.make_async_copy(staying.at[part], out.at[part], sems.at[n]))
+        copies[n].start()
     for copy in copies:
         copy.wait()
 
@@ -438,19 +443,26 @@
 ]
 
 
+answer_shape = (peers * 5, 4, lanes)
+
+
 def sample(received, table):
     return call(
-        sample_kernel, jax.ShapeDtypeStruct((peers * 5, 4, lanes), f32), [vmem] * 2, 24,
-        unpack_scratch + [pltpu.VMEM((bins * 40, lanes), f32), pltpu.SemaphoreType.DMA],
+        sample_kernel, pltpu.HBM(answer_shape, f32), [vmem] * 2, 24,
+        unpack_scratch
+        + [pltpu.VMEM((bins * 40, lanes), f32), pltpu.VMEM(answer_shape, f32),
+           pltpu.SemaphoreType.DMA((quarters + 1,))],
+        hbm,
     )(received, table)
 
 
 def deposit(results, received):
     return call(
-        deposit_kernel, shape(5 * plane), [vmem, vmem], 24,
-        unpack_scratch
-        + [pltpu.VMEM((blocks * 40, lanes), f32), pltpu.VMEM((bins * 8, lanes), f32), pltpu.SemaphoreType.DMA],
-    )(results, received)
+        deposit_kernel, shape(5 * plane), [hbm, vmem], 24,
+        [pltpu.VMEM(answer_shape, f32)] + unpack_scratch
+        + [pltpu.VMEM((blocks * 40, lanes), f32), pltpu.VMEM((bins * 8, lanes), f32),
+           pltpu.SemaphoreType.DMA((2,))],
+    )(pltpu.with_memory_space_constraint(results, pltpu.HBM), received)
 
 
 def advance(gas, sources, halos):
@@ -460,12 +472,18 @@
     )(gas, sources, *halos)
 
 
-def leave(returned, drops, keep, crossing):
-    return call(
-        leave_kernel, [shape(bins * 8), shape(8, moving), shape(8, moving)], [vmem] * 3 + [smem], 16,
-        [pltpu.VMEM((bins * 8, lanes), f32), pltpu.VMEM((bins * 8, lanes), f32), pltpu.SemaphoreType.DMA((4,))],
-        [hbm, vmem, vmem],
-    )(returned, drops, keep, crossing)
+def leave(returned, drops, crossing):
+    return call(
+        leave_kernel, [shape(bins * 8), shape(8, moving), shape(8, moving)], [vmem] * 3, 16,
+        [pltpu.SMEM((2, moving), jnp.int32), pltpu.SemaphoreType.DMA],
+    )(returned, drops, crossing)
+
+
+def stay(updated, keep):
+    return call(
+        stay_kernel, shape(bins * 8), [vmem, vmem], 16,
+        [pltpu.VMEM((bins * 8, lanes), f32), pltpu.SemaphoreType.DMA((quarters,))], hbm,
+    )(updated, keep)
 
 
 def per_device(gas_state, droplets, bin_blocks, bin_counts, crossing):
@@ -489,10 +507,11 @@
     returned = exchange(results)
     gas_next = advance(gas, deposit(results, received), halos)
     returned, gas_next = lax.optimization_barrier((returned, gas_next))
-    kept, toward_next, toward_previous = leave(returned, drops, keep, crossing)
+    updated, toward_next, toward_previous = leave(returned, drops, crossing)
     from_previous = shifted_by(toward_next, "gx", 1)
     from_next = shifted_by(toward_previous, "gx", -1)
     arrivals = jnp.stack([from_previous, from_next], axis=1)
+    kept = stay(updated, keep)
     droplets_next = kept.reshape(bins, 8, lanes).transpose(1, 0, 2).reshape(8, bins * lanes)
     return gas_next.reshape(gas_state.shape), droplets_next, arrivals
 

time: 66.7 us -> 65.1 us (0.976)
  local copies, waits for them, and re-layouts: 4.22 us -> 2.47 us
  Pallas kernels: 22.3 us -> 23.4 us
  waiting for transfers between devices: 12.3 us -> 11.5 us
    unnamed x25 -> x21, local copies, waits for them, and re-layouts: 4.22 us -> 2.47 us
    pallas_call x2 -> x3, Pallas kernels: 9.42 us -> 10.8 us  [the longest x1 6.83 us: deposit(): call(deposit_kernel, shape(5 * plane), [hbm, vmem], 24, [pltpu.VMEM(answe...]
    ppermute x7, waiting for transfers between devices: 7.94 us -> 7.1 us  [shifted_by(): return lax.ppermute(x, axis, [(i, (i + by) % count) for i in range(count)])]
  transfers between devices with their start and end apart: 9 -> 9, of which waited for: 4 -> 4; matrix products, arithmetic and copies ran while one was open for 0% -> 0% of each run, Pallas kernels for 27% -> 30%
where the time goes in v3:
time: 65.1 us; the launch traced here: 64.7 us
  starting transfers between devices  26.5 us (41%)
  Pallas kernels  23.4 us (36%)
  waiting for transfers between devices  11.5 us (18%)
  local copies, waits for them, and re-layouts  2.47 us (4%)
  between operations  0.83 us (1%)
    all_to_all x2, starting transfers between devices, exchange(): return lax.all_to_all(x, 'gx', split_axis=0, concat_axis=0, tiled=True)  19.1 us
    ppermute x7, starting transfers between devices, shifted_by(): return lax.ppermute(x, axis, [(i, (i + by) % count) for i in range(count)])  7.46 us
    ppermute x7, waiting for transfers between devices, shifted_by(): return lax.ppermute(x, axis, [(i, (i + by) % count) for i in range(count)])  7.1 us
    pallas_call x1, Pallas kernels, deposit(): call(deposit_kernel, shape(5 * plane), [hbm, vmem], 24, [pltpu.VMEM(answe...  6.83 us
    pallas_call x1, Pallas kernels, advance(): call(flow_kernel, shape(5 * plane), [vmem] * 7, 24, [pltpu.VMEM((5 * plan...  4.91 us
    all_to_all x2, waiting for transfers between devices, exchange(): return lax.all_to_all(x, 'gx', split_axis=0, concat_axis=0, tiled=True)  4.42 us
    pallas_call x1, Pallas kernels, sample(): call(sample_kernel, pltpu.HBM(answer_shape, f32), [vmem] * 2, 24, unpack_...  3.09 us
    unnamed x21, local copies, waits for them, and re-layouts  2.47 us
  transfers between devices with their start and end apart: 9, of which 4 were waited for; matrix products, arithmetic and copies ran while one was open for 0% of the time, Pallas kernels for 30%

profile of v3, /device:TPU:122, one launch (start us, length us, event | category | flops | bytes accessed | tf_op | source)
XLA Modules:
  0.0 64.7 jit_solution(5600269312344230190)
XLA Ops:
  0.7 2.0 %pack_kernel.1 = f32[288,4,128]{2,1,0:T(4,128)} custom-call(f32[1024,128]{1,0:T(8,128)} %bitcast.19, s32[1,128]{1,0:T(1,128)} %bitcast.27, s32[1,128]{1,0:T(1,128)} %bitcast.21), custom_call_target="tpu_custom_call" | custom-call | tf_op jit(solution)/shard_map/pack_kernel/pallas_call | solution.py:424
  2.7 10.1 %all-to-all-start = ((f32[288,4,128]{2,1,0:T(4,128)}), f32[288,4,128]{2,1,0:T(4,128)S(1)}, u32[]{:S(2)}, u32[]{:S(2)}) async-start(f32[288,4,128]{2,1,0:T(4,128)} %pack_kernel.1), calls=%async_computation | async-start | bytes 1179648 | tf_op jit(solution)/shard_map/all_to_all | solution.py:411
  12.8 1.6 %face_kernel.1 = (f32[240,128]{1,0:T(8,128)}, f32[240,128]{1,0:T(8,128)}, f32[80,128]{1,0:T(8,128)S(1)}, f32[1,1920]{1,0:T(1,128)S(1)}, f32[1,1920]{1,0:T(1,128)S(1)}, /*index=5*/f32[128,128]{1,0:T(8,128)S(1)}) custom-call(f32[1920,128]{1,0:T(8,128)S(1)} %bitcast.16, s32[2,256]{1,0:T(2,128)S(1)} %copy-done.6, s32[1,128]{1,0:T(1,128)S(1)} %bitcast.22), custom_call_target="tpu_custom_call" | custom-call | tf_op jit(solution)/shard_map/face_kernel/pallas_call | solution.py:431
  14.4 0.6 copy-done.2
  15.0 2.7 %collective-permute-start.3 = (f32[240,128]{1,0:T(8,128)}, f32[240,128]{1,0:T(8,128)}, u32[]{:S(2)}, u32[]{:S(2)}) collective-permute-start(f32[240,128]{1,0:T(8,128)} %get-tuple-element.25), channel_id=1, source_target_pairs={{0,4},{4,8},{8,12},{12,16},{16,20},{20,24},{24,28},{28,32},{32,36}... | collective-permute-start | bytes 368648 | tf_op jit(solution)/shard_map/ppermute | solution.py:407
  17.7 0.0 collective-permute-start.4
  17.7 0.0 collective-permute-start
  17.7 1.5 %collective-permute-start.1 = (f32[1,1920]{1,0:T(1,128)S(1)}, f32[1,1920]{1,0:T(1,128)S(1)}, u32[]{:S(2)}, u32[]{:S(2)}) collective-permute-start(f32[1,1920]{1,0:T(1,128)S(1)} %get-tuple-element.22), channel_id=1, source_target_pairs={{0,1},{1,2},{2,3},{3,0},{4,5},{5,6},{6,7},{7,4},{8,9},{9,10},{10,1... | collective-permute-start | bytes 23048 | tf_op jit(solution)/shard_map/ppermute | solution.py:407
  19.2 0.5 collective-permute-start.2
  19.8 2.1 %table_kernel.1.table = bf16[7680,128]{1,0:T(8,128)(2,1)S(1)} custom-call(f32[1920,128]{1,0:T(8,128)S(1)} %bitcast.17), custom_call_target="tpu_custom_call" | custom-call | tf_op jit(solution)/shard_map/table_kernel/pallas_call | solution.py:438
  21.9 0.0 collective-permute-done.1.y_low
  21.9 1.0 %collective-permute-done.2.y_high = f32[1,1920]{1,0:T(1,128)S(1)} collective-permute-done((f32[1,1920]{1,0:T(1,128)S(1)}, f32[1,1920]{1,0:T(1,128)S(1)}, u32[]{:S(2)}, u32[]{:S(2)}) %collective-permute-start.2) | collective-permute-done | bytes 7712 | tf_op jit(solution)/shard_map/ppermute | solution.py:407
  22.9 0.6 copy-done.7
  23.5 0.0 collective-permute-done.z_both
  23.5 0.6 copy-done.4
  24.1 4.4 %all-to-all-done.received = f32[288,4,128]{2,1,0:T(4,128)S(1)} async-done(((f32[288,4,128]{2,1,0:T(4,128)}), f32[288,4,128]{2,1,0:T(4,128)S(1)}, u32[]{:S(2)}, u32[]{:S(2)}) %all-to-all-start) | async-done | bytes 589856 | tf_op jit(solution)/shard_map/all_to_all | solution.py:411
  28.5 3.1 %sample_kernel.1.results = f32[160,4,128]{2,1,0:T(4,128)} custom-call(f32[288,4,128]{2,1,0:T(4,128)S(1)} %all-to-all-done.received, bf16[7680,128]{1,0:T(8,128)(2,1)S(1)} %table_kernel.1.table), custom_call_target="tpu_custom_call" | custom-call | tf_op jit(solution)/shard_map/sample_kernel/pallas_call | solution.py:450
  31.6 0.0 copy-start.8
  31.6 0.0 collective-permute-done.3.x_low
  31.6 0.0 collective-permute-done.4.x_high
  31.6 9.0 %all-to-all-start.1 = ((f32[160,4,128]{2,1,0:T(4,128)}), f32[160,4,128]{2,1,0:T(4,128)S(1)}, u32[]{:S(2)}, u32[]{:S(2)}) async-start(f32[160,4,128]{2,1,0:T(4,128)} %sample_kernel.1.results), calls=%async_computation.1 | async-start | bytes 655360 | tf_op jit(solution)/shard_map/all_to_all | solution.py:411
  40.6 6.8 %deposit_kernel.1.sources = f32[1920,128]{1,0:T(8,128)S(1)} custom-call(f32[160,4,128]{2,1,0:T(4,128)} %sample_kernel.1.results, f32[288,4,128]{2,1,0:T(4,128)S(1)} %all-to-all-done.received), custom_call_target="tpu_custom_call" | custom-call | tf_op jit(solution)/shard_map/deposit_kernel/pallas_call | solution.py:460
  47.5 0.0 copy-start.1
  47.5 4.9 %flow_kernel.1 = f32[1920,128]{1,0:T(8,128)} custom-call(f32[1920,128]{1,0:T(8,128)S(1)} %bitcast.18, f32[1920,128]{1,0:T(8,128)S(1)} %deposit_kernel.1.sources, f32[240,128]{1,0:T(8,128)} %collective-permute-done.3.x_low, f32[240,128]{1,0:T(8,128)} %collective-permute-done.4.x_high, f32[80,128]{1,0:T(8,128)S(1)} %copy-done.5, ...), custom_call_target="tpu_custom_call" | custom-call | tf_op jit(solution)/shard_map/flow_kernel/pallas_call | solution.py:469
  52.4 0.0 all-to-all-done.1.returned
  52.4 2.0 %leave_kernel.1 = (f32[1024,128]{1,0:T(8,128)S(1)}, f32[8,256]{1,0:T(8,128)S(1)}, f32[8,256]{1,0:T(8,128)S(1)}) custom-call(f32[160,4,128]{2,1,0:T(4,128)S(1)} %all-to-all-done.1.returned, f32[1024,128]{1,0:T(8,128)S(1)} %bitcast.20, s32[2,256]{1,0:T(2,128)S(1)} %copy-done.6), custom_call_target="tpu_custom_call" | custom-call | tf_op jit(solution)/shard_map/leave_kernel/pallas_call | solution.py:476
  54.4 2.7 %collective-permute-start.5 = (f32[8,256]{1,0:T(8,128)S(1)}, f32[8,256]{1,0:T(8,128)S(1)}, u32[]{:S(2)}, u32[]{:S(2)}) collective-permute-start(f32[8,256]{1,0:T(8,128)S(1)} %get-tuple-element.37), channel_id=1, source_target_pairs={{0,4},{4,8},{8,12},{12,16},{16,20},{20,24},{24,28},{28,32},{32,36}... | collective-permute-start | bytes 24584 | tf_op jit(solution)/shard_map/ppermute | solution.py:407
  57.2 0.0 collective-permute-start.6
  57.2 0.8 %stay_kernel.1 = f32[1024,128]{1,0:T(8,128)} custom-call(f32[1024,128]{1,0:T(8,128)S(1)} %get-tuple-element.35.updated, f32[128,128]{1,0:T(8,128)S(1)} %copy-done.3), custom_call_target="tpu_custom_call" | custom-call | tf_op jit(solution)/shard_map/stay_kernel/pallas_call | solution.py:483
  58.0 0.5 collective-permute-done.5
  58.5 5.6 %collective-permute-done.6 = f32[8,256]{1,0:T(8,128)S(1)} collective-permute-done((f32[8,256]{1,0:T(8,128)S(1)}, f32[8,256]{1,0:T(8,128)S(1)}, u32[]{:S(2)}, u32[]{:S(2)}) %collective-permute-start.6) | collective-permute-done | bytes 8224 | tf_op jit(solution)/shard_map/ppermute | solution.py:407
  64.1 0.6 copy.8
  (16 shorter events, 0.0 us)
Async XLA Ops:
  0.6 12.2 %copy-start.9 = (s32[128]{0:T(128)S(1)}, s32[128]{0:T(128)}, u32[]{:S(2)}) copy-start(s32[128]{0:T(128)} %param.8) | copy-start | bytes 1540
  0.6 12.2 %copy-start.6 = (s32[2,256]{1,0:T(2,128)S(1)}, s32[2,256]{1,0:T(2,128)}, u32[]{:S(2)}) copy-start(s32[2,256]{1,0:T(2,128)} %crossing.3) | copy-start | bytes 6148
  0.7 12.2 %copy-start = (f32[5,8,48,128]{3,2,1,0:T(8,128)S(1)}, f32[5,8,48,128]{3,2,1,0:T(8,128)}, u32[]{:S(2)}) copy-start(f32[5,8,48,128]{3,2,1,0:T(8,128)} %param.5) | copy-start | bytes 2949124
  2.7 25.8 %all-to-all-start = ((f32[288,4,128]{2,1,0:T(4,128)}), f32[288,4,128]{2,1,0:T(4,128)S(1)}, u32[]{:S(2)}, u32[]{:S(2)}) async-start(f32[288,4,128]{2,1,0:T(4,128)} %pack_kernel.1), calls=%async_computation | async-start | bytes 1179648 | tf_op jit(solution)/shard_map/all_to_all | solution.py:411
  14.4 0.6 copy-start.2
  15.0 16.6 %collective-permute-start.3 = (f32[240,128]{1,0:T(8,128)}, f32[240,128]{1,0:T(8,128)}, u32[]{:S(2)}, u32[]{:S(2)}) collective-permute-start(f32[240,128]{1,0:T(8,128)} %get-tuple-element.25), channel_id=1, source_target_pairs={{0,4},{4,8},{8,12},{12,16},{16,20},{20,24},{24,28},{28,32},{32,36}... | collective-permute-start | bytes 368648 | tf_op jit(solution)/shard_map/ppermute | solution.py:407
  17.7 13.9 %collective-permute-start.4 = (f32[240,128]{1,0:T(8,128)}, f32[240,128]{1,0:T(8,128)}, u32[]{:S(2)}, u32[]{:S(2)}) collective-permute-start(f32[240,128]{1,0:T(8,128)} %get-tuple-element.26), channel_id=1, source_target_pairs={{0,124},{4,0},{8,4},{12,8},{16,12},{20,16},{24,20},{28,24},{32,28}... | collective-permute-start | bytes 368648 | tf_op jit(solution)/shard_map/ppermute | solution.py:407
  17.7 5.7 %collective-permute-start = (f32[80,128]{1,0:T(8,128)S(1)}, f32[80,128]{1,0:T(8,128)S(1)}, u32[]{:S(2)}, u32[]{:S(2)}) collective-permute-start(f32[80,128]{1,0:T(8,128)S(1)} %get-tuple-element.21), channel_id=1, source_target_pairs={{0,128},{128,0},{1,129},{129,1},{2,130},{130,2},{3,131},{131,3},{4... | collective-permute-start | bytes 122888 | tf_op jit(solution)/shard_map/ppermute | solution.py:407
  17.7 4.2 %collective-permute-start.1 = (f32[1,1920]{1,0:T(1,128)S(1)}, f32[1,1920]{1,0:T(1,128)S(1)}, u32[]{:S(2)}, u32[]{:S(2)}) collective-permute-start(f32[1,1920]{1,0:T(1,128)S(1)} %get-tuple-element.22), channel_id=1, source_target_pairs={{0,1},{1,2},{2,3},{3,0},{4,5},{5,6},{6,7},{7,4},{8,9},{9,10},{10,1... | collective-permute-start | bytes 23048 | tf_op jit(solution)/shard_map/ppermute | solution.py:407
  19.2 3.6 %collective-permute-start.2 = (f32[1,1920]{1,0:T(1,128)S(1)}, f32[1,1920]{1,0:T(1,128)S(1)}, u32[]{:S(2)}, u32[]{:S(2)}) collective-permute-start(f32[1,1920]{1,0:T(1,128)S(1)} %get-tuple-element.23), channel_id=1, source_target_pairs={{0,3},{1,0},{2,1},{3,2},{4,7},{5,4},{6,5},{7,6},{8,11},{9,8},{10,9... | collective-permute-start | bytes 23048 | tf_op jit(solution)/shard_map/ppermute | solution.py:407
  22.9 0.6 copy-start.7
  23.5 0.6 copy-start.4
  31.6 15.9 %copy-start.5 = (f32[80,128]{1,0:T(8,128)S(1)}, f32[80,128]{1,0:T(8,128)}, u32[]{:S(2)}) copy-start(f32[80,128]{1,0:T(8,128)} %copy-done.4) | copy-start | bytes 122884
  31.6 15.9 %copy-start.8 = (f32[1,1920]{1,0:T(1,128)S(1)}, f32[1,1920]{1,0:T(1,128)}, u32[]{:S(2)}) copy-start(f32[1,1920]{1,0:T(1,128)} %copy-done.7) | copy-start | bytes 23044
  31.6 20.8 %all-to-all-start.1 = ((f32[160,4,128]{2,1,0:T(4,128)}), f32[160,4,128]{2,1,0:T(4,128)S(1)}, u32[]{:S(2)}, u32[]{:S(2)}) async-start(f32[160,4,128]{2,1,0:T(4,128)} %sample_kernel.1.results), calls=%async_computation.1 | async-start | bytes 655360 | tf_op jit(solution)/shard_map/all_to_all | solution.py:411
  47.5 4.9 %copy-start.1 = (f32[8,16384]{1,0:T(8,128)S(1)}, f32[8,16384]{1,0:T(8,128)}, u32[]{:S(2)}) copy-start(f32[8,16384]{1,0:T(8,128)} %param.6) | copy-start | bytes 1572868
  47.5 9.7 %copy-start.3 = (f32[128,128]{1,0:T(8,128)S(1)}, f32[128,128]{1,0:T(8,128)}, u32[]{:S(2)}) copy-start(f32[128,128]{1,0:T(8,128)} %copy-done.2) | copy-start | bytes 196612
  54.4 4.1 %collective-permute-start.5 = (f32[8,256]{1,0:T(8,128)S(1)}, f32[8,256]{1,0:T(8,128)S(1)}, u32[]{:S(2)}, u32[]{:S(2)}) collective-permute-start(f32[8,256]{1,0:T(8,128)S(1)} %get-tuple-element.37), channel_id=1, source_target_pairs={{0,4},{4,8},{8,12},{12,16},{16,20},{20,24},{24,28},{28,32},{32,36}... | collective-permute-start | bytes 24584 | tf_op jit(solution)/shard_map/ppermute | solution.py:407
  57.2 7.0 %collective-permute-start.6 = (f32[8,256]{1,0:T(8,128)S(1)}, f32[8,256]{1,0:T(8,128)S(1)}, u32[]{:S(2)}, u32[]{:S(2)}) collective-permute-start(f32[8,256]{1,0:T(8,128)S(1)} %get-tuple-element.38), channel_id=1, source_target_pairs={{0,124},{4,0},{8,4},{12,8},{16,12},{20,16},{24,20},{28,24},{32,28}... | collective-permute-start | bytes 24584 | tf_op jit(solution)/shard_map/ppermute | solution.py:407

commit v4 on v3

--- a/solution.py
+++ b/solution.py
@@ -358,39 +358,33 @@
     lax.fori_loop(0, depth, layer, 0)
 
 
-def leave_kernel(returned, drops, crossing, updated, toward_next, toward_previous, slots, sem):
-    copy = pltpu.make_async_copy(crossing, slots, sem)
-    copy.start()
+def leave_kernel(returned, drops, crossing, updated, toward_next, toward_previous):
     for g in range(bins // 8):
         values = group_values(returned, g)
         places = [drops[pl.ds(g * 64 + a, 8, stride=8), :] + 0.2 * values[a] for a in range(3)]
         for n, value in enumerate(places + values):
-            updated[pl.ds(g * 64 + n, 8, stride=8), :] = value
-    copy.wait()
-
-    lane = lane_index(8)
-
-    def batch(s, carry):
-        tiles = list(carry)
-        for e in range(per_batch):
-            for t in range(4):
-                target = s * per_batch + e
-                slot = slots[t // 2, (t % 2) * lanes + target]
-                tile = updated[pl.ds(pl.multiple_of((slot >> 7) * 8, 8), 8), :]
-                moved = pltpu.roll(tile, (target - slot) & (lanes - 1), 1)
-                tiles[t] = jnp.where(lane == target, moved, tiles[t])
-        return tuple(tiles)
-
-    tiles = lax.fori_loop(0, lanes // per_batch, batch, (jnp.zeros((8, lanes), f32),) * 4)
-    toward_next[...] = jnp.concatenate(tiles[0:2], axis=1)
-    toward_previous[...] = jnp.concatenate(tiles[2:4], axis=1)
+            updated[n * bins + g * 8 : n * bins + g * 8 + 8, :] = value
+    row = lax.broadcasted_iota(jnp.int32, (bins, moving), 0)
+    dims = (((0,), (0,)), ((), ()))
+    for side, out in ((0, toward_next), (1, toward_previous)):
+        slots = crossing[side : side + 1, :]
+        in_bin = jnp.where(row == (slots >> 7), 1.0, 0.0).astype(bf16)
+        in_lane = row == (slots & (lanes - 1))
+        for n in range(8):
+            high, low = split(updated[n * bins : (n + 1) * bins, :])
+            picked = lax.dot_general(high, in_bin, dims, preferred_element_type=f32)
+            picked += lax.dot_general(low, in_bin, dims, preferred_element_type=f32)
+            out[n : n + 1, :] = jnp.sum(jnp.where(in_lane, picked, 0.0), axis=0, keepdims=True)
 
 
 def stay_kernel(updated, keep, out, staying, sems):
     copies = []
     for n in range(quarters):
-        for b in range(n * 32, n * 32 + 32):
-            staying[b * 8 : (b + 1) * 8, :] = updated[b * 8 : (b + 1) * 8, :] * keep[b : b + 1, :]
+        for g in range(n * 4, n * 4 + 4):
+            mask = keep[g * 8 : (g + 1) * 8, :]
+            for v in range(8):
+                plane_rows = updated[v * bins + g * 8 : v * bins + g * 8 + 8, :]
+                staying[pl.ds(g * 64 + v, 8, stride=8), :] = plane_rows * mask
         part = pl.ds(n * 256, 256)
         copies.append(pltpu.make_async_copy(staying.at[part], out.at[part], sems.at[n]))
         copies[n].start()
@@ -474,8 +468,7 @@
 
 def leave(returned, drops, crossing):
     return call(
-        leave_kernel, [shape(bins * 8), shape(8, moving), shape(8, moving)], [vmem] * 3, 16,
-        [pltpu.SMEM((2, moving), jnp.int32), pltpu.SemaphoreType.DMA],
+        leave_kernel, [shape(bins * 8), shape(8, moving), shape(8, moving)], [vmem] * 3, 16
     )(returned, drops, crossing)
 
 

time: 65.1 us -> 63.9 us (0.982)
  Pallas kernels: 23.4 us -> 22.2 us
    pallas_call x1, Pallas kernels: 2 us -> 0.79 us  [leave(): call(leave_kernel, [shape(bins * 8), shape(8, moving), shape(8, moving)],...]
  transfers between devices with their start and end apart: 9 -> 9, of which waited for: 4 -> 4; matrix products, arithmetic and copies ran while one was open for 0% -> 0% of each run, Pallas kernels for 30% -> 31%
where the time goes in v4:
time: 63.9 us; the launch traced here: 63.5 us
  starting transfers between devices  26.6 us (42%)
  Pallas kernels  22.2 us (35%)
  waiting for transfers between devices  11.5 us (18%)
  local copies, waits for them, and re-layouts  2.47 us (4%)
  between operations  0.82 us (1%)
    all_to_all x2, starting transfers between devices, exchange(): return lax.all_to_all(x, 'gx', split_axis=0, concat_axis=0, tiled=True)  19.1 us
    ppermute x7, starting transfers between devices, shifted_by(): return lax.ppermute(x, axis, [(i, (i + by) % count) for i in range(count)])  7.45 us
    ppermute x7, waiting for transfers between devices, shifted_by(): return lax.ppermute(x, axis, [(i, (i + by) % count) for i in range(count)])  7.09 us
    pallas_call x1, Pallas kernels, deposit(): call(deposit_kernel, shape(5 * plane), [hbm, vmem], 24, [pltpu.VMEM(answe...  6.83 us
    pallas_call x1, Pallas kernels, advance(): call(flow_kernel, shape(5 * plane), [vmem] * 7, 24, [pltpu.VMEM((5 * plan...  4.91 us
    all_to_all x2, waiting for transfers between devices, exchange(): return lax.all_to_all(x, 'gx', split_axis=0, concat_axis=0, tiled=True)  4.42 us
    pallas_call x1, Pallas kernels, sample(): call(sample_kernel, pltpu.HBM(answer_shape, f32), [vmem] * 2, 24, unpack_...  3.09 us
    unnamed x21, local copies, waits for them, and re-layouts  2.47 us
  transfers between devices with their start and end apart: 9, of which 4 were waited for; matrix products, arithmetic and copies ran while one was open for 0% of the time, Pallas kernels for 31%

profile of v4, /device:TPU:122, one launch (start us, length us, event | category | flops | bytes accessed | tf_op | source)
XLA Modules:
  0.0 63.5 jit_solution(2370698023128882701)
XLA Ops:
  0.7 2.0 %pack_kernel.1 = f32[288,4,128]{2,1,0:T(4,128)} custom-call(f32[1024,128]{1,0:T(8,128)} %bitcast.19, s32[1,128]{1,0:T(1,128)} %bitcast.27, s32[1,128]{1,0:T(1,128)} %bitcast.21), custom_call_target="tpu_custom_call" | custom-call | tf_op jit(solution)/shard_map/pack_kernel/pallas_call | solution.py:418
  2.7 10.1 %all-to-all-start = ((f32[288,4,128]{2,1,0:T(4,128)}), f32[288,4,128]{2,1,0:T(4,128)S(1)}, u32[]{:S(2)}, u32[]{:S(2)}) async-start(f32[288,4,128]{2,1,0:T(4,128)} %pack_kernel.1), calls=%async_computation | async-start | bytes 1179648 | tf_op jit(solution)/shard_map/all_to_all | solution.py:405
  12.8 1.6 %face_kernel.1 = (f32[240,128]{1,0:T(8,128)}, f32[240,128]{1,0:T(8,128)}, f32[80,128]{1,0:T(8,128)S(1)}, f32[1,1920]{1,0:T(1,128)S(1)}, f32[1,1920]{1,0:T(1,128)S(1)}, /*index=5*/f32[128,128]{1,0:T(8,128)S(1)}) custom-call(f32[1920,128]{1,0:T(8,128)S(1)} %bitcast.16, s32[2,256]{1,0:T(2,128)S(1)} %copy-done.6, s32[1,128]{1,0:T(1,128)S(1)} %bitcast.22), custom_call_target="tpu_custom_call" | custom-call | tf_op jit(solution)/shard_map/face_kernel/pallas_call | solution.py:425
  14.4 0.6 copy-done.2
  15.0 2.7 %collective-permute-start.3 = (f32[240,128]{1,0:T(8,128)}, f32[240,128]{1,0:T(8,128)}, u32[]{:S(2)}, u32[]{:S(2)}) collective-permute-start(f32[240,128]{1,0:T(8,128)} %get-tuple-element.25), channel_id=1, source_target_pairs={{0,4},{4,8},{8,12},{12,16},{16,20},{20,24},{24,28},{28,32},{32,36}... | collective-permute-start | bytes 368648 | tf_op jit(solution)/shard_map/ppermute | solution.py:401
  17.7 0.0 collective-permute-start.4
  17.7 0.0 collective-permute-start
  17.7 1.5 %collective-permute-start.1 = (f32[1,1920]{1,0:T(1,128)S(1)}, f32[1,1920]{1,0:T(1,128)S(1)}, u32[]{:S(2)}, u32[]{:S(2)}) collective-permute-start(f32[1,1920]{1,0:T(1,128)S(1)} %get-tuple-element.22), channel_id=1, source_target_pairs={{0,1},{1,2},{2,3},{3,0},{4,5},{5,6},{6,7},{7,4},{8,9},{9,10},{10,1... | collective-permute-start | bytes 23048 | tf_op jit(solution)/shard_map/ppermute | solution.py:401
  19.2 0.5 collective-permute-start.2
  19.8 2.1 %table_kernel.1.table = bf16[7680,128]{1,0:T(8,128)(2,1)S(1)} custom-call(f32[1920,128]{1,0:T(8,128)S(1)} %bitcast.17), custom_call_target="tpu_custom_call" | custom-call | tf_op jit(solution)/shard_map/table_kernel/pallas_call | solution.py:432
  21.9 0.0 collective-permute-done.1.y_low
  21.9 1.0 %collective-permute-done.2.y_high = f32[1,1920]{1,0:T(1,128)S(1)} collective-permute-done((f32[1,1920]{1,0:T(1,128)S(1)}, f32[1,1920]{1,0:T(1,128)S(1)}, u32[]{:S(2)}, u32[]{:S(2)}) %collective-permute-start.2) | collective-permute-done | bytes 7712 | tf_op jit(solution)/shard_map/ppermute | solution.py:401
  22.9 0.6 copy-done.7
  23.5 0.0 collective-permute-done.z_both
  23.5 0.6 copy-done.4
  24.1 4.4 %all-to-all-done.received = f32[288,4,128]{2,1,0:T(4,128)S(1)} async-done(((f32[288,4,128]{2,1,0:T(4,128)}), f32[288,4,128]{2,1,0:T(4,128)S(1)}, u32[]{:S(2)}, u32[]{:S(2)}) %all-to-all-start) | async-done | bytes 589856 | tf_op jit(solution)/shard_map/all_to_all | solution.py:405
  28.5 3.1 %sample_kernel.1.results = f32[160,4,128]{2,1,0:T(4,128)} custom-call(f32[288,4,128]{2,1,0:T(4,128)S(1)} %all-to-all-done.received, bf16[7680,128]{1,0:T(8,128)(2,1)S(1)} %table_kernel.1.table), custom_call_target="tpu_custom_call" | custom-call | tf_op jit(solution)/shard_map/sample_kernel/pallas_call | solution.py:444
  31.6 0.0 copy-start.8
  31.6 0.0 collective-permute-done.3.x_low
  31.6 0.0 collective-permute-done.4.x_high
  31.6 9.0 %all-to-all-start.1 = ((f32[160,4,128]{2,1,0:T(4,128)}), f32[160,4,128]{2,1,0:T(4,128)S(1)}, u32[]{:S(2)}, u32[]{:S(2)}) async-start(f32[160,4,128]{2,1,0:T(4,128)} %sample_kernel.1.results), calls=%async_computation.1 | async-start | bytes 655360 | tf_op jit(solution)/shard_map/all_to_all | solution.py:405
  40.6 6.8 %deposit_kernel.1.sources = f32[1920,128]{1,0:T(8,128)S(1)} custom-call(f32[160,4,128]{2,1,0:T(4,128)} %sample_kernel.1.results, f32[288,4,128]{2,1,0:T(4,128)S(1)} %all-to-all-done.received), custom_call_target="tpu_custom_call" | custom-call | tf_op jit(solution)/shard_map/deposit_kernel/pallas_call | solution.py:454
  47.5 0.0 copy-start.1
  47.5 4.9 %flow_kernel.1 = f32[1920,128]{1,0:T(8,128)} custom-call(f32[1920,128]{1,0:T(8,128)S(1)} %bitcast.18, f32[1920,128]{1,0:T(8,128)S(1)} %deposit_kernel.1.sources, f32[240,128]{1,0:T(8,128)} %collective-permute-done.3.x_low, f32[240,128]{1,0:T(8,128)} %collective-permute-done.4.x_high, f32[80,128]{1,0:T(8,128)S(1)} %copy-done.5, ...), custom_call_target="tpu_custom_call" | custom-call | tf_op jit(solution)/shard_map/flow_kernel/pallas_call | solution.py:463
  52.4 0.0 all-to-all-done.1.returned
  52.4 0.8 %leave_kernel.1 = (f32[1024,128]{1,0:T(8,128)S(1)}, f32[8,256]{1,0:T(8,128)S(1)}, f32[8,256]{1,0:T(8,128)S(1)}) custom-call(f32[160,4,128]{2,1,0:T(4,128)S(1)} %all-to-all-done.1.returned, f32[1024,128]{1,0:T(8,128)S(1)} %bitcast.20, s32[2,256]{1,0:T(2,128)S(1)} %copy-done.6), custom_call_target="tpu_custom_call" | custom-call | tf_op jit(solution)/shard_map/leave_kernel/pallas_call | solution.py:470
  53.2 2.7 %collective-permute-start.5 = (f32[8,256]{1,0:T(8,128)S(1)}, f32[8,256]{1,0:T(8,128)S(1)}, u32[]{:S(2)}, u32[]{:S(2)}) collective-permute-start(f32[8,256]{1,0:T(8,128)S(1)} %get-tuple-element.37), channel_id=1, source_target_pairs={{0,4},{4,8},{8,12},{12,16},{16,20},{20,24},{24,28},{28,32},{32,36}... | collective-permute-start | bytes 24584 | tf_op jit(solution)/shard_map/ppermute | solution.py:401
  56.0 0.0 collective-permute-start.6
  56.0 0.8 %stay_kernel.1 = f32[1024,128]{1,0:T(8,128)} custom-call(f32[1024,128]{1,0:T(8,128)S(1)} %get-tuple-element.35.updated, f32[128,128]{1,0:T(8,128)S(1)} %copy-done.3), custom_call_target="tpu_custom_call" | custom-call | tf_op jit(solution)/shard_map/stay_kernel/pallas_call | solution.py:476
  56.8 0.5 collective-permute-done.5
  57.3 5.6 %collective-permute-done.6 = f32[8,256]{1,0:T(8,128)S(1)} collective-permute-done((f32[8,256]{1,0:T(8,128)S(1)}, f32[8,256]{1,0:T(8,128)S(1)}, u32[]{:S(2)}, u32[]{:S(2)}) %collective-permute-start.6) | collective-permute-done | bytes 8224 | tf_op jit(solution)/shard_map/ppermute | solution.py:401
  62.9 0.6 copy.8
  (16 shorter events, 0.0 us)
Async XLA Ops:
  0.6 12.2 %copy-start.9 = (s32[128]{0:T(128)S(1)}, s32[128]{0:T(128)}, u32[]{:S(2)}) copy-start(s32[128]{0:T(128)} %param.8) | copy-start | bytes 1540
  0.6 12.2 %copy-start.6 = (s32[2,256]{1,0:T(2,128)S(1)}, s32[2,256]{1,0:T(2,128)}, u32[]{:S(2)}) copy-start(s32[2,256]{1,0:T(2,128)} %crossing.3) | copy-start | bytes 6148
  0.7 12.2 %copy-start = (f32[5,8,48,128]{3,2,1,0:T(8,128)S(1)}, f32[5,8,48,128]{3,2,1,0:T(8,128)}, u32[]{:S(2)}) copy-start(f32[5,8,48,128]{3,2,1,0:T(8,128)} %param.5) | copy-start | bytes 2949124
  2.7 25.8 %all-to-all-start = ((f32[288,4,128]{2,1,0:T(4,128)}), f32[288,4,128]{2,1,0:T(4,128)S(1)}, u32[]{:S(2)}, u32[]{:S(2)}) async-start(f32[288,4,128]{2,1,0:T(4,128)} %pack_kernel.1), calls=%async_computation | async-start | bytes 1179648 | tf_op jit(solution)/shard_map/all_to_all | solution.py:405
  14.4 0.6 copy-start.2
  15.0 16.6 %collective-permute-start.3 = (f32[240,128]{1,0:T(8,128)}, f32[240,128]{1,0:T(8,128)}, u32[]{:S(2)}, u32[]{:S(2)}) collective-permute-start(f32[240,128]{1,0:T(8,128)} %get-tuple-element.25), channel_id=1, source_target_pairs={{0,4},{4,8},{8,12},{12,16},{16,20},{20,24},{24,28},{28,32},{32,36}... | collective-permute-start | bytes 368648 | tf_op jit(solution)/shard_map/ppermute | solution.py:401
  17.7 13.9 %collective-permute-start.4 = (f32[240,128]{1,0:T(8,128)}, f32[240,128]{1,0:T(8,128)}, u32[]{:S(2)}, u32[]{:S(2)}) collective-permute-start(f32[240,128]{1,0:T(8,128)} %get-tuple-element.26), channel_id=1, source_target_pairs={{0,124},{4,0},{8,4},{12,8},{16,12},{20,16},{24,20},{28,24},{32,28}... | collective-permute-start | bytes 368648 | tf_op jit(solution)/shard_map/ppermute | solution.py:401
  17.7 5.7 %collective-permute-start = (f32[80,128]{1,0:T(8,128)S(1)}, f32[80,128]{1,0:T(8,128)S(1)}, u32[]{:S(2)}, u32[]{:S(2)}) collective-permute-start(f32[80,128]{1,0:T(8,128)S(1)} %get-tuple-element.21), channel_id=1, source_target_pairs={{0,128},{128,0},{1,129},{129,1},{2,130},{130,2},{3,131},{131,3},{4... | collective-permute-start | bytes 122888 | tf_op jit(solution)/shard_map/ppermute | solution.py:401
  17.7 4.2 %collective-permute-start.1 = (f32[1,1920]{1,0:T(1,128)S(1)}, f32[1,1920]{1,0:T(1,128)S(1)}, u32[]{:S(2)}, u32[]{:S(2)}) collective-permute-start(f32[1,1920]{1,0:T(1,128)S(1)} %get-tuple-element.22), channel_id=1, source_target_pairs={{0,1},{1,2},{2,3},{3,0},{4,5},{5,6},{6,7},{7,4},{8,9},{9,10},{10,1... | collective-permute-start | bytes 23048 | tf_op jit(solution)/shard_map/ppermute | solution.py:401
  19.2 3.6 %collective-permute-start.2 = (f32[1,1920]{1,0:T(1,128)S(1)}, f32[1,1920]{1,0:T(1,128)S(1)}, u32[]{:S(2)}, u32[]{:S(2)}) collective-permute-start(f32[1,1920]{1,0:T(1,128)S(1)} %get-tuple-element.23), channel_id=1, source_target_pairs={{0,3},{1,0},{2,1},{3,2},{4,7},{5,4},{6,5},{7,6},{8,11},{9,8},{10,9... | collective-permute-start | bytes 23048 | tf_op jit(solution)/shard_map/ppermute | solution.py:401
  22.9 0.6 copy-start.7
  23.5 0.6 copy-start.4
  31.6 15.9 %copy-start.5 = (f32[80,128]{1,0:T(8,128)S(1)}, f32[80,128]{1,0:T(8,128)}, u32[]{:S(2)}) copy-start(f32[80,128]{1,0:T(8,128)} %copy-done.4) | copy-start | bytes 122884
  31.6 15.9 %copy-start.8 = (f32[1,1920]{1,0:T(1,128)S(1)}, f32[1,1920]{1,0:T(1,128)}, u32[]{:S(2)}) copy-start(f32[1,1920]{1,0:T(1,128)} %copy-done.7) | copy-start | bytes 23044
  31.6 20.8 %all-to-all-start.1 = ((f32[160,4,128]{2,1,0:T(4,128)}), f32[160,4,128]{2,1,0:T(4,128)S(1)}, u32[]{:S(2)}, u32[]{:S(2)}) async-start(f32[160,4,128]{2,1,0:T(4,128)} %sample_kernel.1.results), calls=%async_computation.1 | async-start | bytes 655360 | tf_op jit(solution)/shard_map/all_to_all | solution.py:405
  47.5 4.9 %copy-start.1 = (f32[8,16384]{1,0:T(8,128)S(1)}, f32[8,16384]{1,0:T(8,128)}, u32[]{:S(2)}) copy-start(f32[8,16384]{1,0:T(8,128)} %param.6) | copy-start | bytes 1572868
  47.5 8.5 %copy-start.3 = (f32[128,128]{1,0:T(8,128)S(1)}, f32[128,128]{1,0:T(8,128)}, u32[]{:S(2)}) copy-start(f32[128,128]{1,0:T(8,128)} %copy-done.2) | copy-start | bytes 196612
  53.2 4.1 %collective-permute-start.5 = (f32[8,256]{1,0:T(8,128)S(1)}, f32[8,256]{1,0:T(8,128)S(1)}, u32[]{:S(2)}, u32[]{:S(2)}) collective-permute-start(f32[8,256]{1,0:T(8,128)S(1)} %get-tuple-element.37), channel_id=1, source_target_pairs={{0,4},{4,8},{8,12},{12,16},{16,20},{20,24},{24,28},{28,32},{32,36}... | collective-permute-start | bytes 24584 | tf_op jit(solution)/shard_map/ppermute | solution.py:401
  56.0 7.0 %collective-permute-start.6 = (f32[8,256]{1,0:T(8,128)S(1)}, f32[8,256]{1,0:T(8,128)S(1)}, u32[]{:S(2)}, u32[]{:S(2)}) collective-permute-start(f32[8,256]{1,0:T(8,128)S(1)} %get-tuple-element.38), channel_id=1, source_target_pairs={{0,124},{4,0},{8,4},{12,8},{16,12},{20,16},{24,20},{28,24},{32,28}... | collective-permute-start | bytes 24584 | tf_op jit(solution)/shard_map/ppermute | solution.py:401
